TPU v7x, 32 devices: a whole 2x2x4 slice. The times are simulated.
32 devices in a mesh: fsdp: 8 (over z, y), tp: 4 (over x, core).
Axes of the slice: x: 2, y: 2, z: 4, core: 2. Of those that a mesh axis runs over, the one named last changes fastest.
Arguments:
- tokens: bfloat16 [8192, 1024], P(('fsdp', 'tp')), may hold values from -6 to 6
- segment_ids: int32 [8192], P('fsdp'), may hold values from 0 to 127, as said below
- cotangent: bfloat16 [8192, 1024], P(('fsdp', 'tp')), may hold values from -6 to 6
- norm_gain: float32 [1024], P(('fsdp', 'tp')), may hold values from 0.5 to 1.5
- w_z: float32 [1024, 1536], P('fsdp', 'tp'), may hold values from -0.09375 to 0.09375, as said below
- w_x: float32 [1024, 1536], P('fsdp', 'tp'), may hold values from -0.09375 to 0.09375, as said below
- w_bc: float32 [1024, 256], P(('fsdp', 'tp')), may hold values from -0.09375 to 0.09375, as said below
- w_dt: float32 [1024, 24], P('fsdp', 'tp'), may hold values from -0.09375 to 0.09375, as said below
- conv_x: float32 [1536, 4], P('tp'), may hold values from -3 to 3
- conv_bias_x: float32 [1536], P('tp'), may hold values from -1.75 to 1.75
- conv_bc: float32 [256, 4], P(('fsdp', 'tp')), may hold values from -3 to 3
- conv_bias_bc: float32 [256], P(('fsdp', 'tp')), may hold values from -1.75 to 1.75
- dt_bias: float32 [24], P('tp'), may hold values from -6 to -2
- a_log: float32 [24], P('tp'), may hold values from 0 to 2.75
- d_skip: float32 [24], P('tp'), may hold values from 0.5 to 1.5
- mixer_gain: float32 [1536], P('tp'), may hold values from 0.5 to 1.5
- w_mixer_out: float32 [1536, 1024], P('tp', 'fsdp'), may hold values from -0.15625 to 0.15625
- w_query: float32 [1024, 512], P('fsdp', 'tp'), may hold values from -0.09375 to 0.09375, as said below
- w_keyval: float32 [1024, 256], P(('fsdp', 'tp')), may hold values from -0.09375 to 0.09375, as said below
- w_attn_out: float32 [512, 1024], P('tp', 'fsdp'), may hold values from -0.75 to 0.75
- ffn_gain: float32 [1024], P(('fsdp', 'tp')), may hold values from 0.5 to 1.5
- w_gate: float32 [1024, 2048], P('fsdp', 'tp'), may hold values from -0.1875 to 0.1875
- w_up: float32 [1024, 2048], P('fsdp', 'tp'), may hold values from -0.1875 to 0.1875
- w_down: float32 [2048, 1024], P('tp', 'fsdp'), may hold values from -0.125 to 0.125
Outputs:
- layer_out: bfloat16 [8192, 1024], P(('fsdp', 'tp'))
- grad_tokens: float32 [8192, 1024], P(('fsdp', 'tp'))
- grad_norm_gain: float32 [1024], P(('fsdp', 'tp'))
- grad_w_z: float32 [1024, 1536], P('fsdp', 'tp')
- grad_w_x: float32 [1024, 1536], P('fsdp', 'tp')
- grad_w_bc: float32 [1024, 256], P(('fsdp', 'tp'))
- grad_w_dt: float32 [1024, 24], P('fsdp', 'tp')
- grad_conv_x: float32 [1536, 4], P('tp')
- grad_conv_bias_x: float32 [1536], P('tp')
- grad_conv_bc: float32 [256, 4], P(('fsdp', 'tp'))
- grad_conv_bias_bc: float32 [256], P(('fsdp', 'tp'))
- grad_dt_bias: float32 [24], P('tp')
- grad_a_log: float32 [24], P('tp')
- grad_d_skip: float32 [24], P('tp')
- grad_mixer_gain: float32 [1536], P('tp')
- grad_w_mixer_out: float32 [1536, 1024], P('tp', 'fsdp')
- grad_w_query: float32 [1024, 512], P('fsdp', 'tp')
- grad_w_keyval: float32 [1024, 256], P(('fsdp', 'tp'))
- grad_w_attn_out: float32 [512, 1024], P('tp', 'fsdp')
- grad_ffn_gain: float32 [1024], P(('fsdp', 'tp'))
- grad_w_gate: float32 [1024, 2048], P('fsdp', 'tp')
- grad_w_up: float32 [1024, 2048], P('fsdp', 'tp')
- grad_w_down: float32 [2048, 1024], P('tp', 'fsdp')
Inputs may be any that keep to these rules, and one draw needn't show every extreme that they name: `segment_ids`: within each sequence of 1024 tokens the ids start at 0 and rise by 0 or 1 from one token to the next; they rise only at positions that are multiples of 8 within the sequence. `w_z`: independent entries of deviation 1024^-0.5. `w_x`: independent entries of deviation 1024^-0.5. `w_bc`: independent entries of deviation 1024^-0.5. `w_dt`: independent entries of deviation 1024^-0.5. `w_query`: independent entries of deviation 1024^-0.5. `w_keyval`: independent entries of deviation 1024^-0.5.
All inputs are finite; a program needn't handle non-finite values.
Results may differ from a plain program's by a relative error of at most 0.025.
Values may be sent and summed in bfloat16 or wider, within the bound.
No kernel may reach another device: no remote copies, remote signals or barrier semaphores. Data moves between devices by JAX's collectives and lax.ppermute only.
A program may use at most 192 MiB of HBM per device.

v0:
```python
import jax
import jax.numpy as jnp
from jax import lax
from jax.sharding import PartitionSpec as P

STATE = 128
CONV = 4
HEADS = 8
KV_HEADS = 2
HEAD = 64
SEQ = 1024


EPS = 1e-06
ROPE_BASE = 10000.0
NEG_FILL = -1e30


def sequence_tables(seg_ids):
    length = seg_ids.shape[0]
    places = jnp.arange(length, dtype=jnp.int32)
    before = jnp.roll(seg_ids, 1)
    starts = jnp.where((places == 0) | (seg_ids != before), places, 0)
    position = places - lax.cummax(starts, axis=0)
    half_dim = HEAD // 2
    frequency = jnp.exp(-jnp.log(ROPE_BASE) * jnp.arange(half_dim, dtype=jnp.float32) / half_dim)
    angles = position.astype(jnp.float32)[:, None] * frequency[None, :]
    cosine = jnp.cos(angles)[:, None, :]
    sine_vals = jnp.sin(angles)[:, None, :]
    causal = (seg_ids[:, None] == seg_ids[None, :]) & (places[:, None] >= places[None, :])
    conv_keep = [
        ((places >= lag_step) & (seg_ids == jnp.roll(seg_ids, lag_step)))[:, None]
        for lag_step in range(1, CONV)
    ]
    return (cosine, sine_vals, causal, conv_keep)


def rotate(values, cosine, sine_vals):
    half_dim = values.shape[-1] // 2
    first_half = values[..., :half_dim]
    second_half = values[..., half_dim:]
    return jnp.concatenate(
        [
            first_half * cosine - second_half * sine_vals,
            second_half * cosine + first_half * sine_vals,
        ],
        axis=-1,
    )


def causal_conv(values, kernel, offset, conv_keep):
    kernel_len = kernel.shape[1]
    summed = values * kernel[:, kernel_len - 1] + offset
    for lag_step in range(1, kernel_len):
        shifted = jnp.concatenate(
            [jnp.zeros((lag_step, values.shape[1]), values.dtype), values[:-lag_step]], axis=0
        )
        summed = (
            summed
            + jnp.where(conv_keep[lag_step - 1], shifted, 0.0)
            * kernel[:, kernel_len - 1 - lag_step]
        )
    return summed


def decay_table(log_rates, causal):
    running = jnp.cumsum(log_rates, axis=0).T
    spread = jnp.where(causal[None], running[:, :, None] - running[:, None, :], 0.0)
    return jnp.where(causal[None], jnp.exp(spread), 0.0)


def prepare(
    conv_in,
    state_in,
    step_in,
    kernel_x,
    offset_x,
    kernel_bc,
    offset_bc,
    step_bias,
    rate_log,
    conv_keep,
    causal,
):
    mixer_in = jax.nn.silu(causal_conv(conv_in, kernel_x, offset_x, conv_keep))
    state_act = jax.nn.silu(causal_conv(state_in, kernel_bc, offset_bc, conv_keep))
    step_size = jax.nn.softplus(step_in + step_bias)
    return (mixer_in, state_act, step_size, decay_table(-step_size * jnp.exp(rate_log), causal))


def finish(scan_out, mixed_vals, skip_vec, gate_in, gain_vec):
    seq_len, head_count, head_dim = scan_out.shape
    combined = scan_out + skip_vec[None, :, None] * mixed_vals
    gated_vals = combined * jax.nn.silu(gate_in).reshape(seq_len, head_count, head_dim)
    inverse = lax.rsqrt(jnp.mean(gated_vals * gated_vals, axis=(1, 2), keepdims=True) + EPS)
    return (gated_vals * inverse * gain_vec.reshape(head_count, head_dim)).reshape(
        seq_len, head_count * head_dim
    )


def contract_rows(left_side, right_side):
    return lax.dot_general(
        left_side, right_side, (((0,), (0,)), ((), ())), preferred_element_type=jnp.float32
    )


def contract_cols(left_side, right_side):
    return lax.dot_general(
        left_side, right_side, (((1,), (1,)), ((), ())), preferred_element_type=jnp.float32
    )


def split_cols(matrix, widths):
    pieces = []
    begin_at = 0
    for part_width in widths:
        pieces.append(matrix[:, begin_at : begin_at + part_width])
        begin_at = begin_at + part_width
    return pieces


def gather_rows(rows_in):
    return lax.all_gather(rows_in, "tp", axis=0, tiled=True)


def reduce_rows(rows_in):
    return lax.psum_scatter(
        rows_in.astype(jnp.bfloat16), "tp", scatter_dimension=0, tiled=True
    ).astype(jnp.float32)


def rms_parts(rows_in):
    inverse = lax.rsqrt(jnp.mean(rows_in * rows_in, axis=-1, keepdims=True) + EPS)
    return (rows_in * inverse, inverse)


def rms_back(d_out, normed, inverse, gain_vec):
    scaled = d_out * gain_vec
    d_rows = inverse * (scaled - normed * jnp.mean(scaled * normed, axis=-1, keepdims=True))
    return (d_rows, jnp.sum(d_out * normed, axis=0))


def ssd_core(mixer_in, state_act, step_size, decays):
    seq_len = mixer_in.shape[0]
    head_count = step_size.shape[1]
    mixed_vals = mixer_in.astype(jnp.bfloat16).reshape(seq_len, head_count, -1)
    state_vals = state_act.astype(jnp.bfloat16)
    basis_b = state_vals[:, :STATE]
    basis_c = state_vals[:, STATE:]
    gram_mat = contract_cols(basis_c, basis_b)
    weights_mat = (gram_mat[None] * decays).astype(jnp.bfloat16)
    mixed_f32 = mixed_vals.astype(jnp.float32)
    inputs_mat = (step_size[:, :, None] * mixed_f32).astype(jnp.bfloat16)
    scan_out = jnp.einsum(
        "hts,shp->thp", weights_mat, inputs_mat, preferred_element_type=jnp.float32
    )
    return (mixed_f32, basis_b, basis_c, gram_mat, weights_mat, inputs_mat, scan_out)


def attend_scores(queries, keys_rot, causal):
    products = jnp.einsum(
        "thd,sd->hts", queries, keys_rot, preferred_element_type=jnp.float32
    ) * HEAD ** (-0.5)
    return jnp.where(causal[None], products, NEG_FILL)


def sum_first(stacked):
    return jnp.sum(stacked, axis=0)


def shards(
    tokens,
    segment_ids,
    cotangent,
    norm_gain,
    w_z,
    w_x,
    w_bc,
    w_dt,
    conv_x,
    conv_bias_x,
    conv_bc,
    conv_bias_bc,
    dt_bias,
    a_log,
    d_skip,
    mixer_gain,
    w_mixer_out,
    w_query,
    w_keyval,
    w_attn_out,
    ffn_gain,
    w_gate,
    w_up,
    w_down,
):
    half_type = jnp.bfloat16
    full_type = jnp.float32
    shared = (
        lax.all_gather(norm_gain.astype(half_type), ("fsdp", "tp"), axis=0, tiled=True),
        lax.all_gather(w_bc.astype(half_type), ("fsdp", "tp"), axis=0, tiled=True),
        lax.all_gather(conv_bc.astype(half_type), ("fsdp", "tp"), axis=0, tiled=True),
        lax.all_gather(conv_bias_bc.astype(half_type), ("fsdp", "tp"), axis=0, tiled=True),
        lax.all_gather(w_keyval.astype(half_type), ("fsdp", "tp"), axis=0, tiled=True),
        lax.all_gather(ffn_gain.astype(half_type), ("fsdp", "tp"), axis=0, tiled=True),
    )
    gain_one = shared[0].astype(full_type)
    bc_weight = shared[1]
    kernel_bc = shared[2].astype(full_type)
    offset_bc = shared[3].astype(full_type)
    keyval_all = shared[4]
    gain_two = shared[5].astype(full_type)
    channels = w_z.shape[1]
    query_width = w_query.shape[1]
    query_local = query_width // HEAD
    hidden_local = w_gate.shape[1]
    head_index = lax.axis_index("tp") * query_local // (HEADS // KV_HEADS)
    key_weight = lax.dynamic_slice_in_dim(keyval_all, head_index * HEAD, HEAD, 1)
    value_weight = lax.dynamic_slice_in_dim(keyval_all, (KV_HEADS + head_index) * HEAD, HEAD, 1)
    widths = [channels, channels, 2 * STATE, query_width, HEAD, HEAD]

    def mix_forward(seq_in):
        proj_seq, step_seq, seg_ids = seq_in
        seq_len = proj_seq.shape[0]
        cosine, sine_vals, causal, conv_keep = sequence_tables(seg_ids)
        gate_in, conv_in, state_in, query_raw, key_raw, value_raw = split_cols(proj_seq, widths)
        mixer_in, state_act, step_size, decays = prepare(
            conv_in,
            state_in,
            step_seq,
            conv_x,
            conv_bias_x,
            kernel_bc,
            offset_bc,
            dt_bias,
            a_log,
            conv_keep,
            causal,
        )
        core_out = ssd_core(mixer_in, state_act, step_size, decays)
        mamba_out = finish(core_out[6], core_out[0], d_skip, gate_in, mixer_gain).astype(half_type)
        queries = rotate(query_raw.reshape(seq_len, query_local, HEAD), cosine, sine_vals).astype(
            half_type
        )
        keys_rot = rotate(key_raw.reshape(seq_len, 1, HEAD), cosine, sine_vals)[:, 0].astype(
            half_type
        )
        values_in = value_raw.astype(half_type)
        scores = attend_scores(queries, keys_rot, causal)
        row_max = jnp.max(scores, axis=-1, keepdims=True)
        log_total = row_max + jnp.log(jnp.sum(jnp.exp(scores - row_max), axis=-1, keepdims=True))
        probs_mat = jnp.exp(scores - log_total).astype(half_type)
        attended = jnp.einsum("hts,sd->thd", probs_mat, values_in, preferred_element_type=full_type)
        return (
            mamba_out,
            attended.reshape(seq_len, query_width).astype(half_type),
            log_total[:, :, 0],
        )

    def mix_backward(seq_in):
        proj_seq, step_seq, seg_ids, log_seq, d_cat_seq = seq_in
        seq_len = proj_seq.shape[0]
        cosine, sine_vals, causal, conv_keep = sequence_tables(seg_ids)
        gate_in, conv_in, state_in, query_raw, key_raw, value_raw = split_cols(proj_seq, widths)

        def prep_local(
            conv_part, state_part, step_part, kern_x, offs_x, kern_bc, offs_bc, bias_step, log_rate
        ):
            return prepare(
                conv_part,
                state_part,
                step_part,
                kern_x,
                offs_x,
                kern_bc,
                offs_bc,
                bias_step,
                log_rate,
                conv_keep,
                causal,
            )

        prepared, pull_prep = jax.vjp(
            prep_local,
            conv_in,
            state_in,
            step_seq,
            conv_x,
            conv_bias_x,
            kernel_bc,
            offset_bc,
            dt_bias,
            a_log,
        )
        mixer_in, state_act, step_size, decays = prepared
        mixed_f32, basis_b, basis_c, gram_mat, weights_mat, inputs_mat, scan_out = ssd_core(
            mixer_in, state_act, step_size, decays
        )
        d_mamba = d_cat_seq[:, :channels]
        d_attn = d_cat_seq[:, channels:]
        finished, pull_fin = jax.vjp(finish, scan_out, mixed_f32, d_skip, gate_in, mixer_gain)
        d_scan, d_mixed_skip, grad_skip, d_gate_in, grad_gain = pull_fin(d_mamba)
        d_scan_half = d_scan.astype(half_type)
        d_inputs = jnp.einsum(
            "hts,thp->shp", weights_mat, d_scan_half, preferred_element_type=full_type
        )
        d_weights = jnp.einsum(
            "thp,shp->hts", d_scan_half, inputs_mat, preferred_element_type=full_type
        )
        d_gram = jnp.sum(d_weights * decays, axis=0).astype(half_type)
        d_decays = d_weights * gram_mat[None]
        d_basis_c = jnp.dot(d_gram, basis_b, preferred_element_type=full_type)
        d_basis_b = contract_rows(d_gram, basis_c)
        d_mixed = (d_mixed_skip + d_inputs * step_size[:, :, None]).reshape(seq_len, channels)
        d_step_size = jnp.sum(d_inputs * mixed_f32, axis=-1)
        prep_grads = pull_prep(
            (d_mixed, jnp.concatenate([d_basis_b, d_basis_c], axis=1), d_step_size, d_decays)
        )
        (
            d_conv_in,
            d_state_in,
            d_step_in,
            grad_kx,
            grad_bx,
            grad_kbc,
            grad_bbc,
            grad_sbias,
            grad_rlog,
        ) = prep_grads

        def rope_pair(query_part, key_part):
            return (rotate(query_part, cosine, sine_vals), rotate(key_part, cosine, sine_vals))

        rotated, pull_rope = jax.vjp(
            rope_pair,
            query_raw.reshape(seq_len, query_local, HEAD),
            key_raw.reshape(seq_len, 1, HEAD),
        )
        queries = rotated[0].astype(half_type)
        keys_rot = rotated[1][:, 0].astype(half_type)
        values_in = value_raw.astype(half_type)
        scores = attend_scores(queries, keys_rot, causal)
        probs_full = jnp.exp(scores - log_seq[:, :, None])
        d_attended = d_attn.reshape(seq_len, query_local, HEAD).astype(half_type)
        d_values = jnp.einsum(
            "hts,thd->sd",
            probs_full.astype(half_type),
            d_attended,
            preferred_element_type=full_type,
        )
        d_probs = jnp.einsum("thd,sd->hts", d_attended, values_in, preferred_element_type=full_type)
        d_scores = (
            probs_full * (d_probs - jnp.sum(probs_full * d_probs, axis=-1, keepdims=True))
        ).astype(half_type)
        d_queries = jnp.einsum(
            "hts,sd->thd", d_scores, keys_rot, preferred_element_type=full_type
        ) * HEAD ** (-0.5)
        d_keys = jnp.einsum(
            "hts,thd->sd", d_scores, queries, preferred_element_type=full_type
        ) * HEAD ** (-0.5)
        d_query_raw, d_key_raw = pull_rope((d_queries, d_keys[:, None, :]))
        d_proj = jnp.concatenate(
            [
                d_gate_in,
                d_conv_in,
                d_state_in,
                d_query_raw.reshape(seq_len, query_width),
                d_key_raw.reshape(seq_len, HEAD),
                d_values,
            ],
            axis=1,
        ).astype(half_type)
        return (
            d_proj,
            d_step_in.astype(half_type),
            (grad_kx, grad_bx, grad_kbc, grad_bbc, grad_sbias, grad_rlog, grad_skip, grad_gain),
        )

    gathered = (
        lax.all_gather(w_z.astype(half_type), "fsdp", axis=0, tiled=True),
        lax.all_gather(w_x.astype(half_type), "fsdp", axis=0, tiled=True),
        lax.all_gather(w_dt.astype(half_type), "fsdp", axis=0, tiled=True),
        lax.all_gather(w_query.astype(half_type), "fsdp", axis=0, tiled=True),
        lax.all_gather(w_mixer_out.astype(half_type), "fsdp", axis=1, tiled=True),
        lax.all_gather(w_attn_out.astype(half_type), "fsdp", axis=1, tiled=True),
    )
    proj_weight = jnp.concatenate(
        [gathered[0], gathered[1], bc_weight, gathered[3], key_weight, value_weight], axis=1
    )
    out_weight = jnp.concatenate([gathered[4], gathered[5]], axis=0)
    mixer_fwd = (proj_weight, gathered[2], out_weight)
    group_rows = segment_ids.shape[0]
    seq_count = group_rows // SEQ
    tok_rows = tokens.astype(full_type)
    normed_one, inverse_one = rms_parts(tok_rows)
    first_in = gather_rows((normed_one * gain_one).astype(half_type))
    projected = jnp.dot(first_in, mixer_fwd[0], preferred_element_type=full_type)
    step_raw = jnp.dot(first_in, mixer_fwd[1], preferred_element_type=full_type)
    seg_seqs = segment_ids.reshape(seq_count, SEQ)
    proj_seqs = projected.reshape(seq_count, SEQ, projected.shape[1])
    step_seqs = step_raw.reshape(seq_count, SEQ, step_raw.shape[1])
    mamba_all, attn_all, log_totals = lax.map(mix_forward, (proj_seqs, step_seqs, seg_seqs))
    mixed_cat = jnp.concatenate(
        [mamba_all.reshape(group_rows, channels), attn_all.reshape(group_rows, query_width)], axis=1
    )
    after_mix = tok_rows + reduce_rows(
        jnp.dot(mixed_cat, mixer_fwd[2], preferred_element_type=full_type)
    )
    normed_two, inverse_two = rms_parts(after_mix)
    second_in = gather_rows((normed_two * gain_two).astype(half_type))
    gathered = (
        lax.all_gather(w_gate.astype(half_type), "fsdp", axis=0, tiled=True),
        lax.all_gather(w_up.astype(half_type), "fsdp", axis=0, tiled=True),
        lax.all_gather(w_down.astype(half_type), "fsdp", axis=1, tiled=True),
    )
    ffn_fwd = (jnp.concatenate([gathered[0], gathered[1]], axis=1), gathered[2])
    gate_up = jnp.dot(second_in, ffn_fwd[0], preferred_element_type=full_type)
    gate_out = gate_up[:, :hidden_local]
    up_out = gate_up[:, hidden_local:]
    hidden = (jax.nn.silu(gate_out) * up_out).astype(half_type)
    output = after_mix + reduce_rows(jnp.dot(hidden, ffn_fwd[1], preferred_element_type=full_type))
    cot_all = gather_rows(cotangent)
    d_hidden = contract_cols(cot_all, ffn_fwd[1])
    grad_down = contract_rows(hidden, cot_all)
    gate_sig = jax.nn.sigmoid(gate_out)
    d_gate = d_hidden * up_out * gate_sig * (1.0 + gate_out * (1.0 - gate_sig))
    d_up = d_hidden * (gate_out * gate_sig)
    d_gate_up = jnp.concatenate([d_gate, d_up], axis=1).astype(half_type)
    grad_gate_up = contract_rows(second_in, d_gate_up)
    ffn_sums = (
        lax.psum_scatter(grad_gate_up[:, :hidden_local], "fsdp", scatter_dimension=0, tiled=True),
        lax.psum_scatter(grad_gate_up[:, hidden_local:], "fsdp", scatter_dimension=0, tiled=True),
        lax.psum_scatter(grad_down, "fsdp", scatter_dimension=1, tiled=True),
    )
    d_second = reduce_rows(contract_cols(d_gate_up, ffn_fwd[0]))
    d_norm_two, grad_gain_two = rms_back(d_second, normed_two, inverse_two, gain_two)
    d_after = cotangent.astype(full_type) + d_norm_two
    d_mix_all = gather_rows(d_after.astype(half_type))
    d_cat = contract_cols(d_mix_all, mixer_fwd[2])
    grad_out = contract_rows(mixed_cat, d_mix_all)
    d_projs, d_steps, small_parts = lax.map(
        mix_backward,
        (proj_seqs, step_seqs, seg_seqs, log_totals, d_cat.reshape(seq_count, SEQ, d_cat.shape[1])),
    )
    small_sums = [sum_first(stacked) for stacked in small_parts]
    d_proj_all = d_projs.reshape(group_rows, d_projs.shape[2])
    d_step_all = d_steps.reshape(group_rows, d_steps.shape[2])
    grad_proj = contract_rows(first_in, d_proj_all)
    grad_step = contract_rows(first_in, d_step_all)
    d_first = reduce_rows(
        contract_cols(d_proj_all, mixer_fwd[0]) + contract_cols(d_step_all, mixer_fwd[1])
    )
    d_norm_one, grad_gain_one = rms_back(d_first, normed_one, inverse_one, gain_one)
    grad_tokens = d_after + d_norm_one
    grad_zmat, grad_xmat, grad_bcmat, grad_query, grad_key, grad_value = split_cols(
        grad_proj, widths
    )
    grad_keyval = jnp.zeros((grad_key.shape[0], 2 * KV_HEADS * HEAD), full_type)
    grad_keyval = lax.dynamic_update_slice(grad_keyval, grad_key, (0, head_index * HEAD))
    grad_keyval = lax.dynamic_update_slice(
        grad_keyval, grad_value, (0, (KV_HEADS + head_index) * HEAD)
    )
    mixer_sums = (
        lax.psum_scatter(grad_zmat, "fsdp", scatter_dimension=0, tiled=True),
        lax.psum_scatter(grad_xmat, "fsdp", scatter_dimension=0, tiled=True),
        lax.psum_scatter(grad_step, "fsdp", scatter_dimension=0, tiled=True),
        lax.psum_scatter(grad_query, "fsdp", scatter_dimension=0, tiled=True),
        lax.psum_scatter(grad_out[:channels], "fsdp", scatter_dimension=1, tiled=True),
        lax.psum_scatter(grad_out[channels:], "fsdp", scatter_dimension=1, tiled=True),
    )
    shared_sums = (
        lax.psum_scatter(grad_gain_one, ("fsdp", "tp"), scatter_dimension=0, tiled=True),
        lax.psum_scatter(grad_bcmat, ("fsdp", "tp"), scatter_dimension=0, tiled=True),
        lax.psum_scatter(small_sums[2], ("fsdp", "tp"), scatter_dimension=0, tiled=True),
        lax.psum_scatter(small_sums[3], ("fsdp", "tp"), scatter_dimension=0, tiled=True),
        lax.psum_scatter(grad_keyval, ("fsdp", "tp"), scatter_dimension=0, tiled=True),
        lax.psum_scatter(grad_gain_two, ("fsdp", "tp"), scatter_dimension=0, tiled=True),
    )
    vector_sums = lax.psum(
        (small_sums[0], small_sums[1], small_sums[4], small_sums[5], small_sums[6], small_sums[7]),
        "fsdp",
    )
    return (
        output.astype(half_type),
        grad_tokens,
        shared_sums[0],
        mixer_sums[0],
        mixer_sums[1],
        shared_sums[1],
        mixer_sums[2],
        vector_sums[0],
        vector_sums[1],
        shared_sums[2],
        shared_sums[3],
        vector_sums[2],
        vector_sums[3],
        vector_sums[4],
        vector_sums[5],
        mixer_sums[4],
        mixer_sums[3],
        shared_sums[4],
        mixer_sums[5],
        shared_sums[5],
        ffn_sums[0],
        ffn_sums[1],
        ffn_sums[2],
    )


def solution(mesh):
    placed = (
        P(("fsdp", "tp"), None),
        P("fsdp"),
        P(("fsdp", "tp"), None),
        P(("fsdp", "tp")),
        P("fsdp", "tp"),
        P("fsdp", "tp"),
        P(("fsdp", "tp"), None),
        P("fsdp", "tp"),
        P("tp", None),
        P("tp"),
        P(("fsdp", "tp"), None),
        P(("fsdp", "tp")),
        P("tp"),
        P("tp"),
        P("tp"),
        P("tp"),
        P("tp", "fsdp"),
        P("fsdp", "tp"),
        P(("fsdp", "tp"), None),
        P("tp", "fsdp"),
        P(("fsdp", "tp")),
        P("fsdp", "tp"),
        P("fsdp", "tp"),
        P("tp", "fsdp"),
    )
    return jax.shard_map(
        shards,
        mesh=mesh,
        in_specs=placed,
        out_specs=(
            P(("fsdp", "tp"), None),
            P(("fsdp", "tp"), None),
            P(("fsdp", "tp")),
            P("fsdp", "tp"),
            P("fsdp", "tp"),
            P(("fsdp", "tp"), None),
            P("fsdp", "tp"),
            P("tp", None),
            P("tp"),
            P(("fsdp", "tp"), None),
            P(("fsdp", "tp")),
            P("tp"),
            P("tp"),
            P("tp"),
            P("tp"),
            P("tp", "fsdp"),
            P("fsdp", "tp"),
            P(("fsdp", "tp"), None),
            P("tp", "fsdp"),
            P(("fsdp", "tp")),
            P("fsdp", "tp"),
            P("fsdp", "tp"),
            P("tp", "fsdp"),
        ),
        check_vma=False,
    )
```

profile of v0, /device:TPU:0, one launch (start us, length us, event | category | flops | bytes accessed | tf_op | source)
XLA Modules:
  0.0 1731.3 jit_solution(11487197419187075176)
XLA Ops:
  12.1 42.1 %all-reduce.33 = (bf16[1024]{0:T(1024)(128)(2,1)S(1)}, bf16[256]{0:T(256)(128)(2,1)S(1)}, bf16[1024]{0:T(1024)(128)(2,1)}) all-reduce(bf16[1024]{0:T(1024)(128)(2,1)S(1)} %dynamic-update-slice, bf16[256]{0:T(256)(128)(2,1)S(1)} %dynamic-update-slice.1, ...), channel_id=1, replica_groups=mesh['fsdp'=8,'tp'=4] {'fsdp','tp'}, use_global_device_ids=true, to_apply=%add.24 | all-reduce | flops 2304 | bytes 9216
  57.6 42.1 %all_gather.64 = bf16[1024,256]{1,0:T(8,128)(2,1)S(1)} all-gather(bf16[32,256]{1,0:T(8,128)(2,1)S(1)} %convert_element_type.218), channel_id=1, replica_groups=mesh['fsdp'=8,'tp'=4] {'fsdp','tp'}, dimensions={0}, use_global_device_ids=true | all-gather | bytes 540672 | tf_op jit(solution)/shard_map/all_gather | solution.py:204
  103.8 36.7 %all-gather = bf16[32,8,4]{1,2,0:T(4,128)(2,1)S(1)} all-gather(bf16[1,8,4]{1,2,0:T(4,128)(2,1)S(1)} %convert_bitcast_fusion), channel_id=1, replica_groups=mesh['fsdp'=8,'tp'=4] {'fsdp','tp'}, dimensions={0}, use_global_device_ids=true | all-gather | bytes 2112 | tf_op jit(solution)/shard_map/all_gather | solution.py:202
  145.3 32.8 %all_gather.63 = bf16[1024,128]{1,0:T(8,128)(2,1)} all-gather(bf16[128,128]{1,0:T(8,128)(2,1)S(1)} %convert_element_type.217), channel_id=1, replica_groups=mesh['fsdp'=8,'tp'=4] {'fsdp'}, dimensions={0}, use_global_device_ids=true | all-gather | bytes 294912 | tf_op jit(solution)/shard_map/all_gather | solution.py:383
  179.1 39.4 %all_gather.62 = bf16[1024,256]{1,0:T(8,128)(2,1)S(1)} all-gather(bf16[32,256]{1,0:T(8,128)(2,1)S(1)} %convert_element_type.216), channel_id=1, replica_groups=mesh['fsdp'=8,'tp'=4] {'fsdp','tp'}, dimensions={0}, use_global_device_ids=true | all-gather | bytes 540672 | tf_op jit(solution)/shard_map/all_gather | solution.py:201
  218.5 32.2 %all_gather.61 = bf16[1024,384]{1,0:T(8,128)(2,1)S(1)} all-gather(bf16[128,384]{1,0:T(8,128)(2,1)S(1)} %convert_element_type.215), channel_id=1, replica_groups=mesh['fsdp'=8,'tp'=4] {'fsdp'}, dimensions={0}, use_global_device_ids=true | all-gather | bytes 884736 | tf_op jit(solution)/shard_map/all_gather | solution.py:381
  250.7 32.3 %all_gather.60 = bf16[1024,384]{1,0:T(8,128)(2,1)S(1)} all-gather(bf16[128,384]{1,0:T(8,128)(2,1)} %convert_element_type.214), channel_id=1, replica_groups=mesh['fsdp'=8,'tp'=4] {'fsdp'}, dimensions={0}, use_global_device_ids=true | all-gather | bytes 884736 | tf_op jit(solution)/shard_map/all_gather | solution.py:380
  315.6 26.6 %all_gather.68 = bf16[128,1024]{1,0:T(8,128)(2,1)S(1)} all-gather(bf16[128,128]{1,0:T(8,128)(2,1)} %convert_element_type.238), channel_id=1, replica_groups=mesh['fsdp'=8,'tp'=4] {'fsdp'}, dimensions={1}, use_global_device_ids=true | all-gather | bytes 294912 | tf_op jit(solution)/shard_map/all_gather | solution.py:385
  342.3 27.7 %all_gather.67 = bf16[384,1024]{1,0:T(8,128)(2,1)S(1)} all-gather(bf16[384,128]{1,0:T(8,128)(2,1)S(1)} %convert_element_type.237), channel_id=1, replica_groups=mesh['fsdp'=8,'tp'=4] {'fsdp'}, dimensions={1}, use_global_device_ids=true | all-gather | bytes 884736 | tf_op jit(solution)/shard_map/all_gather | solution.py:384
  472.3 39.2 %all-gather.15.cloned.1.call-done = bf16[1024,512]{1,0:T(8,128)(2,1)} async-done(((bf16[128,512]{1,0:T(8,128)(2,1)}), bf16[1024,512]{1,0:T(8,128)(2,1)}) %all-gather.15.cloned.1.call-update) | async-done | bytes 1048592 | tf_op jit(solution)/shard_map/all_gather | solution.py:413
  541.2 35.7 %all-gather.17.cloned.1.call-done = bf16[512,1024]{1,0:T(8,128)(2,1)} async-done(((bf16[512,128]{1,0:T(8,128)(2,1)}), bf16[512,1024]{1,0:T(8,128)(2,1)}) %all-gather.17.cloned.1.call-update) | async-done | bytes 1048592 | tf_op jit(solution)/shard_map/all_gather | solution.py:414
  611.6 31.3 %reduce-scatter.21.cloned.1.call-done = bf16[256,1024]{1,0:T(8,128)(2,1)} async-done(((bf16[1024,1024]{1,0:T(8,128)(2,1)}), bf16[256,1024]{1,0:T(8,128)(2,1)}) %reduce-scatter.21.cloned.1.call-update) | async-done | bytes 524304 | tf_op jit(solution)/shard_map/reduce_scatter | solution.py:127
  839.4 36.8 %all-reduce.32 = (f32[384,4]{0,1:T(4,128)}, f32[384]{0:T(512)}, f32[6]{0:T(128)}, f32[6]{0:T(128)}, f32[6]{0:T(128)}, /*index=5*/f32[384]{0:T(512)}) all-reduce(f32[384,4]{0,1:T(4,128)S(1)} %pad_add_fusion, f32[384]{0:T(512)S(1)} %copy-done.110, f32[6]{0:T(128)S(1)} %get-tuple-element.178, ...), channel_id=1, replica_groups=mesh['fsdp'=8,'tp'=4] {'fsdp'}, use_global_device_ids=true, to_apply=%region_33.34 | all-reduce | flops 2322 | bytes 18576 | tf_op jit(solution)/shard_map/psum | solution.py:479
  877.9 38.1 %all-reduce.31 = (f32[1024]{0:T(1024)S(1)}, f32[256,4]{0,1:T(4,128)S(1)}, f32[256]{0:T(256)S(1)}, f32[1024]{0:T(1024)S(1)}) all-reduce(f32[1024]{0:T(1024)S(1)} %get-tuple-element.130, f32[256,4]{0,1:T(4,128)S(1)} %pad_add_fusion.2, f32[256]{0:T(256)S(1)} %copy-done.112, ...), channel_id=6, replica_groups=mesh['fsdp'=8,'tp'=4] {'fsdp','tp'}, use_global_device_ids=true, to_apply=%region_24.25.clone | all-reduce | flops 3328 | bytes 26624
  923.0 71.2 %reduce-scatter.41.cloned.1.call-done = f32[128,512]{1,0:T(8,128)} async-done(((f32[1024,512]{1,0:T(8,128)}), f32[128,512]{1,0:T(8,128)}) %reduce-scatter.41.cloned.1.call-update) | async-done | bytes 262160 | tf_op jit(solution)/shard_map/reduce_scatter | solution.py:431
  994.2 71.3 %reduce-scatter.45.cloned.1.call-done = f32[512,128]{1,0:T(8,128)} async-done(((f32[512,1024]{1,0:T(8,128)}), f32[512,128]{1,0:T(8,128)}) %reduce-scatter.45.cloned.1.call-update) | async-done | bytes 262160 | tf_op jit(solution)/shard_map/reduce_scatter | solution.py:433
  1065.5 56.0 %reduce-scatter.31.cloned.1.call-done = f32[128,6]{0,1:T(8,128)} async-done(((f32[1024,6]{0,1:T(8,128)}), f32[128,6]{0,1:T(8,128)}) %reduce-scatter.31.cloned.1.call-update) | async-done | bytes 3088 | tf_op jit(solution)/shard_map/reduce_scatter | solution.py:466
  1121.6 65.5 %reduce-scatter.39.cloned.1.call-done = f32[128,128]{1,0:T(8,128)} async-done(((f32[128,1024]{1,0:T(8,128)}), f32[128,128]{1,0:T(8,128)}) %reduce-scatter.39.cloned.1.call-update) | async-done | bytes 65552 | tf_op jit(solution)/shard_map/reduce_scatter | solution.py:469
  1187.1 65.2 %reduce-scatter.35.cloned.1.call-done = f32[128,128]{1,0:T(8,128)} async-done(((f32[1024,128]{1,0:T(8,128)}), f32[128,128]{1,0:T(8,128)}) %reduce-scatter.35.cloned.1.call-update) | async-done | bytes 65552 | tf_op jit(solution)/shard_map/reduce_scatter | solution.py:467
  1252.3 136.6 %reduce-scatter.29.cloned.1.call-done = f32[32,256]{1,0:T(8,128)} async-done(((f32[1024,256]{1,0:T(8,128)}), f32[32,256]{1,0:T(8,128)}) %reduce-scatter.29.cloned.1.call-update) | async-done | bytes 32784 | tf_op jit(solution)/shard_map/reduce_scatter | solution.py:473
  1388.9 133.5 %reduce-scatter.37.cloned.1.call-done = f32[32,256]{1,0:T(8,128)} async-done(((f32[1024,256]{1,0:T(8,128)}), f32[32,256]{1,0:T(8,128)}) %reduce-scatter.37.cloned.1.call-update) | async-done | bytes 32784 | tf_op jit(solution)/shard_map/reduce_scatter | solution.py:476
  1522.4 65.5 %reduce-scatter.33.cloned.1.call-done = f32[384,128]{1,0:T(8,128)} async-done(((f32[384,1024]{1,0:T(8,128)}), f32[384,128]{1,0:T(8,128)}) %reduce-scatter.33.cloned.1.call-update) | async-done | bytes 196624 | tf_op jit(solution)/shard_map/reduce_scatter | solution.py:468
  1587.9 68.2 %reduce-scatter.27.cloned.1.call-done = f32[128,384]{1,0:T(8,128)} async-done(((f32[1024,384]{1,0:T(8,128)}), f32[128,384]{1,0:T(8,128)}) %reduce-scatter.27.cloned.1.call-update) | async-done | bytes 196624 | tf_op jit(solution)/shard_map/reduce_scatter | solution.py:465
  1656.1 67.8 %reduce-scatter.25.cloned.1.call-done = f32[128,384]{1,0:T(8,128)} async-done(((f32[1024,384]{1,0:T(8,128)}), f32[128,384]{1,0:T(8,128)}) %reduce-scatter.25.cloned.1.call-update) | async-done | bytes 196624 | tf_op jit(solution)/shard_map/reduce_scatter | solution.py:464
  (532 shorter events, 420.0 us)
Async XLA Ops:
  8.1 132.5 %copy-start.59 = (f32[128,128]{1,0:T(8,128)S(1)}, f32[128,128]{1,0:T(8,128)}, u32[]{:S(2)}) copy-start(f32[128,128]{1,0:T(8,128)} %param.41) | copy-start | bytes 196612
  8.1 132.5 %copy-start.60 = (f32[128,128]{1,0:T(8,128)S(1)}, f32[128,128]{1,0:T(8,128)}, u32[]{:S(2)}) copy-start(f32[128,128]{1,0:T(8,128)} %param.43) | copy-start | bytes 196612
  8.1 363.6 %all-gather.9.cloned.1.call-start = ((), (), s32[]{:S(2)}) async-start(), calls=%async_computation.15 | async-start | bytes 2621440 | tf_op jit(solution)/shard_map/all_gather | solution.py:123
  56.3 401.7 %reduce-scatter.17.cloned.1.call-start = ((), (), s32[]{:S(2)}) async-start(), calls=%async_computation.16 | async-start | bytes 2621440 | tf_op jit(solution)/shard_map/reduce_scatter | solution.py:127
  430.1 39.9 %all-gather.13.cloned.1.call-start = ((), (), s32[]{:S(2)}) async-start(), calls=%async_computation.18 | async-start | bytes 1179648 | tf_op jit(solution)/shard_map/all_gather | solution.py:412
  431.8 79.7 %all-gather.15.cloned.1.call-start = ((), (), s32[]{:S(2)}) async-start(), calls=%async_computation.19 | async-start | bytes 1179648 | tf_op jit(solution)/shard_map/all_gather | solution.py:413
  433.5 101.0 %all-gather.11.cloned.1.call-start = ((), (), s32[]{:S(2)}) async-start(), calls=%async_computation.17 | async-start | bytes 2621440 | tf_op jit(solution)/shard_map/all_gather | solution.py:123
  461.9 115.0 %all-gather.17.cloned.1.call-start = ((), (), s32[]{:S(2)}) async-start(), calls=%async_computation.20 | async-start | bytes 1179648 | tf_op jit(solution)/shard_map/all_gather | solution.py:414
  463.6 136.4 %all-gather.19.cloned.1.call-start = ((), (), s32[]{:S(2)}) async-start(), calls=%async_computation.22 | async-start | bytes 2621440 | tf_op jit(solution)/shard_map/all_gather | solution.py:123
  464.4 178.6 %reduce-scatter.21.cloned.1.call-start = ((), (), s32[]{:S(2)}) async-start(), calls=%async_computation.23 | async-start | bytes 2621440 | tf_op jit(solution)/shard_map/reduce_scatter | solution.py:127
  611.4 59.8 %all-gather.21.cloned.1.call-start = ((), (), s32[]{:S(2)}) async-start(), calls=%async_computation.24 | async-start | bytes 2621440 | tf_op jit(solution)/shard_map/all_gather | solution.py:123
  648.5 227.8 %reduce-scatter.23.cloned.1.call-start = ((), (), s32[]{:S(2)}) async-start(), calls=%async_computation.25 | async-start | bytes 2621440 | tf_op jit(solution)/shard_map/reduce_scatter | solution.py:127
  786.0 132.4 %reduce-scatter.19.cloned.1.call-start = ((), (), s32[]{:S(2)}) async-start(), calls=%async_computation.21 | async-start | bytes 2621440 | tf_op jit(solution)/shard_map/reduce_scatter | solution.py:127
  790.2 132.9 %reduce-scatter.43.cloned.1.call-start = ((), (), s32[]{:S(2)}) async-start(), calls=%async_computation.35 | async-start | bytes 2359296 | tf_op jit(solution)/shard_map/reduce_scatter | solution.py:432
  798.5 195.7 %reduce-scatter.41.cloned.1.call-start = ((), (), s32[]{:S(2)}) async-start(), calls=%async_computation.34 | async-start | bytes 2359296 | tf_op jit(solution)/shard_map/reduce_scatter | solution.py:431
  799.1 266.4 %reduce-scatter.45.cloned.1.call-start = ((), (), s32[]{:S(2)}) async-start(), calls=%async_computation.36 | async-start | bytes 2359296 | tf_op jit(solution)/shard_map/reduce_scatter | solution.py:433
  803.9 317.7 %reduce-scatter.31.cloned.1.call-start = ((), (), s32[]{:S(2)}) async-start(), calls=%async_computation.29 | async-start | bytes 36864 | tf_op jit(solution)/shard_map/reduce_scatter | solution.py:466
  806.5 380.6 %reduce-scatter.39.cloned.1.call-start = ((), (), s32[]{:S(2)}) async-start(), calls=%async_computation.33 | async-start | bytes 589824 | tf_op jit(solution)/shard_map/reduce_scatter | solution.py:469
  811.9 440.4 %reduce-scatter.35.cloned.1.call-start = ((), (), s32[]{:S(2)}) async-start(), calls=%async_computation.31 | async-start | bytes 589824 | tf_op jit(solution)/shard_map/reduce_scatter | solution.py:467
  820.1 568.8 %reduce-scatter.29.cloned.1.call-start = ((), (), s32[]{:S(2)}) async-start(), calls=%async_computation.28 | async-start | bytes 1081344 | tf_op jit(solution)/shard_map/reduce_scatter | solution.py:473
  822.5 699.9 %reduce-scatter.37.cloned.1.call-start = ((), (), s32[]{:S(2)}) async-start(), calls=%async_computation.32 | async-start | bytes 1081344 | tf_op jit(solution)/shard_map/reduce_scatter | solution.py:476
  831.5 756.4 %reduce-scatter.33.cloned.1.call-start = ((), (), s32[]{:S(2)}) async-start(), calls=%async_computation.30 | async-start | bytes 1769472 | tf_op jit(solution)/shard_map/reduce_scatter | solution.py:468
  834.3 821.8 %reduce-scatter.27.cloned.1.call-start = ((), (), s32[]{:S(2)}) async-start(), calls=%async_computation.27 | async-start | bytes 1769472 | tf_op jit(solution)/shard_map/reduce_scatter | solution.py:465
  838.4 885.5 %reduce-scatter.25.cloned.1.call-start = ((), (), s32[]{:S(2)}) async-start(), calls=%async_computation.26 | async-start | bytes 1769472 | tf_op jit(solution)/shard_map/reduce_scatter | solution.py:464
  (148 other events, 3091.7 us)
Sparse Core Ops, SparseCore 0:
  56.4 24.7 all-gather.8
  430.2 27.7 reduce-scatter.16
  611.5 31.3 reduce-scatter.20
  648.6 22.5 all-gather.20
Sparse Core Ops, SparseCore 1:
  433.2 36.7 all-gather.12
  472.5 38.9 all-gather.14
  513.6 20.9 all-gather.10
  537.4 39.5 all-gather.16
  578.6 21.4 all-gather.18
  786.0 31.3 reduce-scatter.22
  820.0 31.3 reduce-scatter.18
  855.3 67.7 reduce-scatter.42
  927.0 67.1 reduce-scatter.40
  998.3 67.1 reduce-scatter.44
  1069.1 52.4 reduce-scatter.30
  1125.5 61.5 reduce-scatter.38
  1191.2 61.0 reduce-scatter.34
  1255.1 133.7 reduce-scatter.28
  1391.8 130.5 reduce-scatter.36
  1526.4 61.4 reduce-scatter.32
  1592.3 63.7 reduce-scatter.26
  1660.1 63.7 reduce-scatter.24
where the time goes:
time: 1740 us; the launch traced here: 1730 us
  waiting for transfers between devices  1000 us (57%)
  blocking collectives  413 us (24%)
  matrix products  117 us (7%)
  local copies, waits for them, and re-layouts  94.3 us (5%)
  other arithmetic  85.7 us (5%)
    reduce_scatter x1, waiting for transfers between devices, shards(): lax.psum_scatter(grad_bcmat, ('fsdp', 'tp'), scatter_dimension=0, tiled=T...  137 us
    reduce_scatter x1, waiting for transfers between devices, shards(): lax.psum_scatter(grad_keyval, ('fsdp', 'tp'), scatter_dimension=0, tiled=...  134 us
    unnamed x2, blocking collectives  80.2 us
    reduce_scatter x1, waiting for transfers between devices, shards(): lax.psum_scatter(grad_down, 'fsdp', scatter_dimension=1, tiled=True)  71.3 us
    reduce_scatter x1, waiting for transfers between devices, shards(): lax.psum_scatter(grad_gate_up[:, :hidden_local], 'fsdp', scatter_dimensio...  71.2 us
    reduce_scatter x1, waiting for transfers between devices, shards(): lax.psum_scatter(grad_xmat, 'fsdp', scatter_dimension=0, tiled=True)  68.2 us
    reduce_scatter x1, waiting for transfers between devices, shards(): lax.psum_scatter(grad_zmat, 'fsdp', scatter_dimension=0, tiled=True)  67.8 us
    reduce_scatter x1, waiting for transfers between devices, shards(): lax.psum_scatter(grad_out[:channels], 'fsdp', scatter_dimension=1, tiled=...  65.5 us
  transfers between devices with their start and end apart: 22, of which 19 were waited for; matrix products, arithmetic and copies ran while one was open for 5% of the time, Pallas kernels for 0%

commit v1 on v0

--- a/solution.py
+++ b/solution.py
@@ -119,14 +119,120 @@
     return pieces
 
 
+def flip(values, axis, mask):
+    size = lax.axis_size(axis)
+    return lax.ppermute(values, axis, [(i, i ^ mask) for i in range(size)])
+
+
+def ring(values, step):
+    return lax.ppermute(values, "fsdp", [(i, (i + 2 * step) % 8) for i in range(8)])
+
+
+def staged():
+    return lax.axis_size("fsdp") == 8
+
+
+def place_bits():
+    index = lax.axis_index("tp")
+    return index // 2, index % 2
+
+
 def gather_rows(rows_in):
-    return lax.all_gather(rows_in, "tp", axis=0, tiled=True)
+    x_at, core_at = place_bits()
+    far = flip(rows_in, "tp", 2)
+    near = flip(rows_in, "tp", 1)
+    cross = flip(far, "tp", 1)
+    mine = jnp.where(core_at == 0, jnp.stack([rows_in, near]), jnp.stack([near, rows_in]))
+    theirs = jnp.where(core_at == 0, jnp.stack([far, cross]), jnp.stack([cross, far]))
+    whole = jnp.where(x_at == 0, jnp.stack([mine, theirs]), jnp.stack([theirs, mine]))
+    return whole.reshape(4 * rows_in.shape[0], rows_in.shape[1])
 
 
 def reduce_rows(rows_in):
-    return lax.psum_scatter(
-        rows_in.astype(jnp.bfloat16), "tp", scatter_dimension=0, tiled=True
-    ).astype(jnp.float32)
+    x_at, core_at = place_bits()
+    parts = rows_in.reshape(2, 2, rows_in.shape[0] // 4, rows_in.shape[1])
+    keep = jnp.where(core_at == 0, parts[:, 0], parts[:, 1])
+    give = jnp.where(core_at == 0, parts[:, 1], parts[:, 0]).astype(jnp.bfloat16)
+    half = keep + flip(give, "tp", 1).astype(jnp.float32)
+    keep = jnp.where(x_at == 0, half[0], half[1])
+    give = jnp.where(x_at == 0, half[1], half[0]).astype(jnp.bfloat16)
+    return keep + flip(give, "tp", 2).astype(jnp.float32)
+
+
+def fsdp_place():
+    index = lax.axis_index("fsdp")
+    return index // 2, index % 2
+
+
+def to_rel(values, axis):
+    if not staged():
+        return values
+    z_at, y_at = fsdp_place()
+    shape = values.shape
+    block = shape[axis] // 8
+    split = shape[:axis] + (4, 2, block) + shape[axis + 1 :]
+    parts = values.reshape(split)
+    parts = jnp.where(y_at == 0, parts, jnp.flip(parts, axis + 1))
+    parts = jnp.concatenate([parts, parts], axis)
+    return lax.dynamic_slice_in_dim(parts, z_at, 4, axis).reshape(shape)
+
+
+def from_rel(values, axis):
+    if not staged():
+        return values
+    z_at, y_at = fsdp_place()
+    shape = values.shape
+    block = shape[axis] // 8
+    split = shape[:axis] + (4, 2, block) + shape[axis + 1 :]
+    parts = values.reshape(split)
+    parts = jnp.where(y_at == 0, parts, jnp.flip(parts, axis + 1))
+    parts = jnp.concatenate([parts, parts], axis)
+    return lax.dynamic_slice_in_dim(parts, 4 - z_at, 4, axis).reshape(shape)
+
+
+def gather_fsdp(shard):
+    if not staged():
+        return lax.all_gather(shard, "fsdp", axis=0, tiled=True)
+    rows = shard.shape[0]
+    pair = jnp.concatenate([shard, flip(shard, "fsdp", 1)], axis=0)
+    below = ring(pair, 1)
+    above = ring(pair, -1)
+    far_a = ring(below[:rows], 1)
+    far_b = ring(above[rows:], -1)
+    return jnp.concatenate([pair, above, far_a, far_b, below], axis=0)
+
+
+def scatter_fsdp(grads):
+    if not staged():
+        return lax.psum_scatter(grads, "fsdp", scatter_dimension=0, tiled=True)
+    half_type = jnp.bfloat16
+    rows = grads.shape[0] // 8
+    parts = grads.reshape(4, 2, rows, grads.shape[1])
+    wire = parts.astype(half_type)
+    up_far = ring(wire[2, 0], 1)
+    down_far = ring(wire[2, 1], -1)
+    up_near = ring(wire[1, 1], 1)
+    down_near = ring(wire[3, 0], -1)
+    full = jnp.float32
+    up_sum = ring((parts[1, 0] + up_far.astype(full)).astype(half_type), 1)
+    down_sum = ring((parts[3, 1] + down_far.astype(full)).astype(half_type), -1)
+    own = parts[0, 0] + up_sum.astype(full) + down_near.astype(full)
+    other = parts[0, 1] + up_near.astype(full) + down_sum.astype(full)
+    return own + flip(other.astype(half_type), "fsdp", 1).astype(full)
+
+
+def sum_fsdp(values):
+    if not staged():
+        return lax.psum(values, "fsdp")
+    for mask in (1, 2, 6):
+        values = values + flip(values, "fsdp", mask)
+    return values
+
+
+def sum_tp(values):
+    for mask in (1, 2):
+        values = values + flip(values, "tp", mask)
+    return values
 
 
 def rms_parts(rows_in):
@@ -196,27 +302,38 @@
 ):
     half_type = jnp.bfloat16
     full_type = jnp.float32
-    shared = (
-        lax.all_gather(norm_gain.astype(half_type), ("fsdp", "tp"), axis=0, tiled=True),
-        lax.all_gather(w_bc.astype(half_type), ("fsdp", "tp"), axis=0, tiled=True),
-        lax.all_gather(conv_bc.astype(half_type), ("fsdp", "tp"), axis=0, tiled=True),
-        lax.all_gather(conv_bias_bc.astype(half_type), ("fsdp", "tp"), axis=0, tiled=True),
-        lax.all_gather(w_keyval.astype(half_type), ("fsdp", "tp"), axis=0, tiled=True),
-        lax.all_gather(ffn_gain.astype(half_type), ("fsdp", "tp"), axis=0, tiled=True),
-    )
-    gain_one = shared[0].astype(full_type)
-    bc_weight = shared[1]
-    kernel_bc = shared[2].astype(full_type)
-    offset_bc = shared[3].astype(full_type)
-    keyval_all = shared[4]
-    gain_two = shared[5].astype(full_type)
+    row_count = w_bc.shape[0]
+    gain_rows = norm_gain.shape[0]
+    conv_rows = conv_bc.shape[0]
+    small_in = jnp.concatenate([norm_gain, ffn_gain, conv_bc.reshape(-1), conv_bias_bc])
+    small_size = small_in.shape[0]
+    shared_cols = w_bc.shape[1] + w_keyval.shape[1]
+    small_in = jnp.pad(small_in.reshape(1, -1), ((0, 15), (0, shared_cols - small_size)))
+    shared_in = jnp.concatenate(
+        [jnp.concatenate([w_bc, w_keyval], axis=1), small_in], axis=0
+    ).astype(half_type)
+    shared_all = gather_rows(shared_in).reshape(4, row_count + 16, shared_in.shape[1])
+    small_rows = gather_fsdp(shared_all[:, row_count, :128])
+    small_all = small_rows.reshape(-1, 128)
+    gain_one, gain_two = (
+        small_all[:, at : at + gain_rows].reshape(-1).astype(full_type) for at in (0, gain_rows)
+    )
+    conv_all = from_rel(small_all, 0)[:, 2 * gain_rows : small_size].astype(full_type)
+    kernel_bc = conv_all[:, : conv_rows * CONV].reshape(-1, CONV)
+    offset_bc = conv_all[:, conv_rows * CONV :].reshape(-1)
+    bc_rows = shared_all[:, :row_count].reshape(4 * row_count, shared_in.shape[1])
     channels = w_z.shape[1]
     query_width = w_query.shape[1]
     query_local = query_width // HEAD
     hidden_local = w_gate.shape[1]
     head_index = lax.axis_index("tp") * query_local // (HEADS // KV_HEADS)
-    key_weight = lax.dynamic_slice_in_dim(keyval_all, head_index * HEAD, HEAD, 1)
-    value_weight = lax.dynamic_slice_in_dim(keyval_all, (KV_HEADS + head_index) * HEAD, HEAD, 1)
+    keyval_rows = bc_rows[:, 2 * STATE :]
+    key_rows = jnp.where(head_index == 0, keyval_rows[:, :HEAD], keyval_rows[:, HEAD : 2 * HEAD])
+    value_rows = jnp.where(
+        head_index == 0, keyval_rows[:, 2 * HEAD : 3 * HEAD], keyval_rows[:, 3 * HEAD :]
+    )
+    step_heads = w_dt.shape[1]
+    step_rows = jnp.pad(w_dt.astype(half_type), ((0, 0), (0, 128 - step_heads)))
     widths = [channels, channels, 2 * STATE, query_width, HEAD, HEAD]
 
     def mix_forward(seq_in):
@@ -376,26 +493,39 @@
             (grad_kx, grad_bx, grad_kbc, grad_bbc, grad_sbias, grad_rlog, grad_skip, grad_gain),
         )
 
-    gathered = (
-        lax.all_gather(w_z.astype(half_type), "fsdp", axis=0, tiled=True),
-        lax.all_gather(w_x.astype(half_type), "fsdp", axis=0, tiled=True),
-        lax.all_gather(w_dt.astype(half_type), "fsdp", axis=0, tiled=True),
-        lax.all_gather(w_query.astype(half_type), "fsdp", axis=0, tiled=True),
-        lax.all_gather(w_mixer_out.astype(half_type), "fsdp", axis=1, tiled=True),
-        lax.all_gather(w_attn_out.astype(half_type), "fsdp", axis=1, tiled=True),
-    )
-    proj_weight = jnp.concatenate(
-        [gathered[0], gathered[1], bc_weight, gathered[3], key_weight, value_weight], axis=1
-    )
-    out_weight = jnp.concatenate([gathered[4], gathered[5]], axis=0)
-    mixer_fwd = (proj_weight, gathered[2], out_weight)
+    proj_weight = gather_fsdp(
+        jnp.concatenate(
+            [
+                w_z.astype(half_type),
+                w_x.astype(half_type),
+                bc_rows[:, : 2 * STATE],
+                w_query.astype(half_type),
+                key_rows,
+                value_rows,
+                step_rows,
+            ],
+            axis=1,
+        )
+    )
+    out_weight = gather_fsdp(
+        jnp.concatenate([w_mixer_out.astype(half_type).T, w_attn_out.astype(half_type).T], axis=1)
+    )
+    ffn_weight = gather_fsdp(
+        jnp.concatenate(
+            [w_gate.astype(half_type), w_up.astype(half_type), w_down.astype(half_type).T], axis=1
+        )
+    )
+    gate_up_weight = ffn_weight[:, : 2 * hidden_local]
+    down_weight = ffn_weight[:, 2 * hidden_local :]
     group_rows = segment_ids.shape[0]
     seq_count = group_rows // SEQ
-    tok_rows = tokens.astype(full_type)
+    tok_rows = to_rel(tokens, 1).astype(full_type)
+    cot_rows = to_rel(cotangent, 1)
     normed_one, inverse_one = rms_parts(tok_rows)
     first_in = gather_rows((normed_one * gain_one).astype(half_type))
-    projected = jnp.dot(first_in, mixer_fwd[0], preferred_element_type=full_type)
-    step_raw = jnp.dot(first_in, mixer_fwd[1], preferred_element_type=full_type)
+    projected = jnp.dot(first_in, proj_weight, preferred_element_type=full_type)
+    step_raw = projected[:, sum(widths) : sum(widths) + step_heads]
+    projected = projected[:, : sum(widths)]
     seg_seqs = segment_ids.reshape(seq_count, SEQ)
     proj_seqs = projected.reshape(seq_count, SEQ, projected.shape[1])
     step_seqs = step_raw.reshape(seq_count, SEQ, step_raw.shape[1])
@@ -404,40 +534,30 @@
         [mamba_all.reshape(group_rows, channels), attn_all.reshape(group_rows, query_width)], axis=1
     )
     after_mix = tok_rows + reduce_rows(
-        jnp.dot(mixed_cat, mixer_fwd[2], preferred_element_type=full_type)
+        contract_cols(mixed_cat, out_weight)
     )
     normed_two, inverse_two = rms_parts(after_mix)
     second_in = gather_rows((normed_two * gain_two).astype(half_type))
-    gathered = (
-        lax.all_gather(w_gate.astype(half_type), "fsdp", axis=0, tiled=True),
-        lax.all_gather(w_up.astype(half_type), "fsdp", axis=0, tiled=True),
-        lax.all_gather(w_down.astype(half_type), "fsdp", axis=1, tiled=True),
-    )
-    ffn_fwd = (jnp.concatenate([gathered[0], gathered[1]], axis=1), gathered[2])
-    gate_up = jnp.dot(second_in, ffn_fwd[0], preferred_element_type=full_type)
+    gate_up = jnp.dot(second_in, gate_up_weight, preferred_element_type=full_type)
     gate_out = gate_up[:, :hidden_local]
     up_out = gate_up[:, hidden_local:]
     hidden = (jax.nn.silu(gate_out) * up_out).astype(half_type)
-    output = after_mix + reduce_rows(jnp.dot(hidden, ffn_fwd[1], preferred_element_type=full_type))
-    cot_all = gather_rows(cotangent)
-    d_hidden = contract_cols(cot_all, ffn_fwd[1])
-    grad_down = contract_rows(hidden, cot_all)
+    output = after_mix + reduce_rows(contract_cols(hidden, down_weight))
+    cot_all = gather_rows(cot_rows)
+    d_hidden = jnp.dot(cot_all, down_weight, preferred_element_type=full_type)
+    grad_down = contract_rows(cot_all, hidden)
     gate_sig = jax.nn.sigmoid(gate_out)
     d_gate = d_hidden * up_out * gate_sig * (1.0 + gate_out * (1.0 - gate_sig))
     d_up = d_hidden * (gate_out * gate_sig)
     d_gate_up = jnp.concatenate([d_gate, d_up], axis=1).astype(half_type)
     grad_gate_up = contract_rows(second_in, d_gate_up)
-    ffn_sums = (
-        lax.psum_scatter(grad_gate_up[:, :hidden_local], "fsdp", scatter_dimension=0, tiled=True),
-        lax.psum_scatter(grad_gate_up[:, hidden_local:], "fsdp", scatter_dimension=0, tiled=True),
-        lax.psum_scatter(grad_down, "fsdp", scatter_dimension=1, tiled=True),
-    )
-    d_second = reduce_rows(contract_cols(d_gate_up, ffn_fwd[0]))
+    ffn_sum = scatter_fsdp(jnp.concatenate([grad_gate_up, grad_down], axis=1))
+    d_second = reduce_rows(contract_cols(d_gate_up, gate_up_weight))
     d_norm_two, grad_gain_two = rms_back(d_second, normed_two, inverse_two, gain_two)
-    d_after = cotangent.astype(full_type) + d_norm_two
+    d_after = cot_rows.astype(full_type) + d_norm_two
     d_mix_all = gather_rows(d_after.astype(half_type))
-    d_cat = contract_cols(d_mix_all, mixer_fwd[2])
-    grad_out = contract_rows(mixed_cat, d_mix_all)
+    d_cat = jnp.dot(d_mix_all, out_weight, preferred_element_type=full_type)
+    out_sum = scatter_fsdp(contract_rows(d_mix_all, mixed_cat))
     d_projs, d_steps, small_parts = lax.map(
         mix_backward,
         (proj_seqs, step_seqs, seg_seqs, log_totals, d_cat.reshape(seq_count, SEQ, d_cat.shape[1])),
@@ -445,65 +565,80 @@
     small_sums = [sum_first(stacked) for stacked in small_parts]
     d_proj_all = d_projs.reshape(group_rows, d_projs.shape[2])
     d_step_all = d_steps.reshape(group_rows, d_steps.shape[2])
-    grad_proj = contract_rows(first_in, d_proj_all)
-    grad_step = contract_rows(first_in, d_step_all)
-    d_first = reduce_rows(
-        contract_cols(d_proj_all, mixer_fwd[0]) + contract_cols(d_step_all, mixer_fwd[1])
-    )
+    d_wide = jnp.concatenate(
+        [d_proj_all, jnp.pad(d_step_all, ((0, 0), (0, 128 - step_heads)))], axis=1
+    )
+    proj_sum = scatter_fsdp(contract_rows(first_in, d_wide))
+    d_first = reduce_rows(contract_cols(d_wide, proj_weight))
     d_norm_one, grad_gain_one = rms_back(d_first, normed_one, inverse_one, gain_one)
-    grad_tokens = d_after + d_norm_one
-    grad_zmat, grad_xmat, grad_bcmat, grad_query, grad_key, grad_value = split_cols(
-        grad_proj, widths
-    )
-    grad_keyval = jnp.zeros((grad_key.shape[0], 2 * KV_HEADS * HEAD), full_type)
-    grad_keyval = lax.dynamic_update_slice(grad_keyval, grad_key, (0, head_index * HEAD))
-    grad_keyval = lax.dynamic_update_slice(
-        grad_keyval, grad_value, (0, (KV_HEADS + head_index) * HEAD)
-    )
-    mixer_sums = (
-        lax.psum_scatter(grad_zmat, "fsdp", scatter_dimension=0, tiled=True),
-        lax.psum_scatter(grad_xmat, "fsdp", scatter_dimension=0, tiled=True),
-        lax.psum_scatter(grad_step, "fsdp", scatter_dimension=0, tiled=True),
-        lax.psum_scatter(grad_query, "fsdp", scatter_dimension=0, tiled=True),
-        lax.psum_scatter(grad_out[:channels], "fsdp", scatter_dimension=1, tiled=True),
-        lax.psum_scatter(grad_out[channels:], "fsdp", scatter_dimension=1, tiled=True),
-    )
-    shared_sums = (
-        lax.psum_scatter(grad_gain_one, ("fsdp", "tp"), scatter_dimension=0, tiled=True),
-        lax.psum_scatter(grad_bcmat, ("fsdp", "tp"), scatter_dimension=0, tiled=True),
-        lax.psum_scatter(small_sums[2], ("fsdp", "tp"), scatter_dimension=0, tiled=True),
-        lax.psum_scatter(small_sums[3], ("fsdp", "tp"), scatter_dimension=0, tiled=True),
-        lax.psum_scatter(grad_keyval, ("fsdp", "tp"), scatter_dimension=0, tiled=True),
-        lax.psum_scatter(grad_gain_two, ("fsdp", "tp"), scatter_dimension=0, tiled=True),
-    )
-    vector_sums = lax.psum(
-        (small_sums[0], small_sums[1], small_sums[4], small_sums[5], small_sums[6], small_sums[7]),
-        "fsdp",
-    )
+    grad_tokens = from_rel(d_after + d_norm_one, 1)
+    sum_z, sum_x, sum_bc, sum_query, sum_key, sum_value, sum_step = split_cols(
+        proj_sum, widths + [step_heads]
+    )
+
+    x_at, core_at = place_bits()
+    shared_rows = jnp.concatenate([sum_bc, sum_key, sum_value], axis=1)
+    shared_rows = shared_rows.reshape(2, 2, row_count, shared_rows.shape[1])
+    keep = jnp.where(core_at == 0, shared_rows[:, 0], shared_rows[:, 1])
+    give = jnp.where(core_at == 0, shared_rows[:, 1], shared_rows[:, 0])
+    chip_rows = keep + flip(give, "tp", 1)
+    keep = jnp.where(x_at == 0, chip_rows[0], chip_rows[1])
+    give = jnp.where(x_at == 0, chip_rows[1], chip_rows[0])
+    came = flip(give, "tp", 2)
+    grad_bc = keep[:, : 2 * STATE] + came[:, : 2 * STATE]
+    key_mine, value_mine = split_cols(keep[:, 2 * STATE :], [HEAD, HEAD])
+    key_came, value_came = split_cols(came[:, 2 * STATE :], [HEAD, HEAD])
+    grad_keyval = jnp.where(
+        x_at == 0,
+        jnp.concatenate([key_mine, key_came, value_mine, value_came], axis=1),
+        jnp.concatenate([key_came, key_mine, value_came, value_mine], axis=1),
+    )
+
+    gains = jnp.stack([from_rel(grad_gain_one, 0), from_rel(grad_gain_two, 0)])
+    common = jnp.concatenate([gains.reshape(-1), small_sums[2].reshape(-1), small_sums[3]])
+    common_size = common.shape[0]
+    parts = [small_sums[0], small_sums[1], small_sums[4], small_sums[5], small_sums[6], small_sums[7]]
+    flat = jnp.concatenate([sum_tp(common)] + [part.reshape(-1) for part in parts])
+    flat = jnp.pad(flat, (0, -flat.shape[0] % 1024)).reshape(-1, 128)
+    flat = sum_fsdp(flat).reshape(-1)
+    vector_sums = []
+    begin_at = common_size
+    for part in parts:
+        vector_sums.append(flat[begin_at : begin_at + part.size].reshape(part.shape))
+        begin_at = begin_at + part.size
+    device = lax.axis_index("fsdp") * 4 + lax.axis_index("tp")
+    width = grad_gain_one.shape[0]
+    sum_gain_one = lax.dynamic_slice_in_dim(flat[:width], device * gain_rows, gain_rows)
+    sum_gain_two = lax.dynamic_slice_in_dim(flat[width : 2 * width], device * gain_rows, gain_rows)
+    conv_flat = flat[2 * width : 2 * width + 2 * STATE * CONV].reshape(2 * STATE, CONV)
+    bias_flat = flat[2 * width + 2 * STATE * CONV : common_size]
+    sum_conv = lax.dynamic_slice_in_dim(conv_flat, device * conv_rows, conv_rows)
+    sum_bias = lax.dynamic_slice_in_dim(bias_flat, device * conv_rows, conv_rows)
+    sum_gate, sum_up, sum_down = split_cols(ffn_sum, [hidden_local, hidden_local, hidden_local])
     return (
-        output.astype(half_type),
+        from_rel(output.astype(half_type), 1),
         grad_tokens,
-        shared_sums[0],
-        mixer_sums[0],
-        mixer_sums[1],
-        shared_sums[1],
-        mixer_sums[2],
+        sum_gain_one,
+        sum_z,
+        sum_x,
+        grad_bc,
+        sum_step,
         vector_sums[0],
         vector_sums[1],
-        shared_sums[2],
-        shared_sums[3],
+        sum_conv,
+        sum_bias,
         vector_sums[2],
         vector_sums[3],
         vector_sums[4],
         vector_sums[5],
-        mixer_sums[4],
-        mixer_sums[3],
-        shared_sums[4],
-        mixer_sums[5],
-        shared_sums[5],
-        ffn_sums[0],
-        ffn_sums[1],
-        ffn_sums[2],
+        out_sum[:, :channels].T,
+        sum_query,
+        grad_keyval,
+        out_sum[:, channels:].T,
+        sum_gain_two,
+        sum_gate,
+        sum_up,
+        sum_down.T,
     )
 
 

time: 1740 us -> 639 us (0.37)
  waiting for transfers between devices: 1000 us -> 179 us
  blocking collectives: 413 us -> 0 us
  starting transfers between devices: 1.34 us -> 80.7 us
  other arithmetic: 85.7 us -> 134 us
  local copies, waits for them, and re-layouts: 94.3 us -> 134 us
  matrix products: 117 us -> 97.3 us
    reduce_scatter x15 -> x0, waiting for transfers between devices: 857 us -> none  [the longest x1 137 us: shards(): lax.psum_scatter(grad_bcmat, ('fsdp', 'tp'), scatter_dimension=0, tiled=T...]
    all_gather x9 -> x0, blocking collectives: 296 us -> none  [the longest x1 42.1 us: shards(): lax.all_gather(w_keyval.astype(half_type), ('fsdp', 'tp'), axis=0, tiled=...]
    ppermute x0 -> x71, waiting for transfers between devices: none -> 179 us  [the longest x34 129 us: ring(): lax.ppermute(values, 'fsdp', [(i, (i + 2 * step) % 8) for i in range(8)])]
    all_gather x7 -> x0, waiting for transfers between devices: 143 us -> none  [the longest x4 62.8 us: gather_rows(): return lax.all_gather(rows_in, 'tp', axis=0, tiled=True)]
    ppermute x0 -> x71, starting transfers between devices: none -> 80.7 us  [the longest x34 54.4 us: ring(): lax.ppermute(values, 'fsdp', [(i, (i + 2 * step) % 8) for i in range(8)])]
    unnamed x2 -> x0, blocking collectives: 80.2 us -> none
    psum x1 -> x0, blocking collectives: 36.8 us -> none  [shards(): lax.psum((small_sums[0], small_sums[1], small_sums[4], small_sums[5], sma...]
    reshape x0 -> x17, local copies, waits for them, and re-layouts: none -> 22.9 us  [the longest x3 14.5 us: scatter_fsdp(): parts = grads.reshape(4, 2, rows, grads.shape[1])]
  transfers between devices with their start and end apart: 22 -> 71, of which waited for: 19 -> 31; matrix products, arithmetic and copies ran while one was open for 5% -> 42% of each run, Pallas kernels for 0% -> 0%
where the time goes in v1:
time: 639 us; the launch traced here: 629 us
  waiting for transfers between devices  179 us (28%)
  local copies, waits for them, and re-layouts  134 us (21%)
  other arithmetic  134 us (21%)
  matrix products  97.3 us (15%)
  starting transfers between devices  80.7 us (13%)
    ppermute x34, waiting for transfers between devices, ring(): lax.ppermute(values, 'fsdp', [(i, (i + 2 * step) % 8) for i in range(8)])  129 us
    ppermute x34, starting transfers between devices, ring(): lax.ppermute(values, 'fsdp', [(i, (i + 2 * step) % 8) for i in range(8)])  54.4 us
    ppermute x37, waiting for transfers between devices, flip(): return lax.ppermute(values, axis, [(i, i ^ mask) for i in range(size)])  49.7 us
    unnamed x360, local copies, waits for them, and re-layouts  31.4 us
    ppermute x37, starting transfers between devices, flip(): return lax.ppermute(values, axis, [(i, i ^ mask) for i in range(size)])  26.3 us
    another operation x13, other arithmetic  18.5 us
    dot_general x1, matrix products, mix_backward(): jnp.einsum('thp,shp->hts', d_scan_half, inputs_mat, preferred_element_typ...  17.3 us
    dot_general x5, matrix products, contract_cols(): lax.dot_general(left_side, right_side, (((1,), (1,)), ((), ())), preferre...  15.4 us
  transfers between devices with their start and end apart: 71, of which 31 were waited for; matrix products, arithmetic and copies ran while one was open for 42% of the time, Pallas kernels for 0%

profile of v1, /device:TPU:0, one launch (start us, length us, event | category | flops | bytes accessed | tf_op | source)
XLA Modules:
  0.0 628.5 jit_solution(1809259957928279355)
XLA Ops:
  66.4 5.1 collective-permute-done.18
  92.2 9.0 %collective-permute-done.13 = bf16[256,1408]{1,0:T(8,128)(2,1)S(1)} collective-permute-done((bf16[256,1408]{1,0:T(8,128)(2,1)S(1)}, bf16[256,1408]{1,0:T(8,128)(2,1)S(1)}, u32[]{:S(2)}, u32[]{:S(2)}) %collective-permute-start.13) | collective-permute-done | bytes 720928 | tf_op jit(solution)/shard_map/ppermute | solution.py:128
  101.7 13.2 %collective-permute-done.12 = bf16[256,1408]{1,0:T(8,128)(2,1)S(1)} collective-permute-done((bf16[256,1408]{1,0:T(8,128)(2,1)S(1)}, bf16[256,1408]{1,0:T(8,128)(2,1)S(1)}, u32[]{:S(2)}, u32[]{:S(2)}) %collective-permute-start.12) | collective-permute-done | bytes 720928 | tf_op jit(solution)/shard_map/ppermute | solution.py:128
  119.0 8.4 %collective-permute-done.14 = bf16[128,1408]{1,0:T(8,128)(2,1)S(1)} collective-permute-done((bf16[128,1408]{1,0:T(8,128)(2,1)S(1)}, bf16[128,1408]{1,0:T(8,128)(2,1)S(1)}, u32[]{:S(2)}, u32[]{:S(2)}) %collective-permute-start.14) | collective-permute-done | bytes 360480 | tf_op jit(solution)/shard_map/ppermute | solution.py:128
  163.2 11.0 %multiply_reduce_fusion.8 = (f32[1024]{0:T(1024)S(1)}, f32[1024,6,64]{0,2,1:T(8,128)S(1)}, f32[1024,6,64]{0,2,1:T(8,128)}) fusion(f32[1024,6,64]{0,2,1:T(8,128)S(1)} %bitcast.537, f32[1024,6,64]{0,2,1:T(8,128)} %bitcast.562, f32[6]{0:T(128)S(1)} %copy-done.146, f32[6,1024]{1,0:T(8,128)S(1)} %bitcast.598, f32[1024,1024]{1,0:T(8,128)} %fusion.107, ...), kind=kOutput, calls=%fused_computation.85 | convolution fusion | flops 839515136 | bytes 11587608 | tf_op jit(solution)/shard_map/while/body/eval_jaxpr/hts,shp->thp/dot_general | solution.py:260
  229.4 12.6 %collective-permute-done.27 = bf16[256,1536]{0,1:T(8,128)(2,1)} collective-permute-done((bf16[256,1536]{0,1:T(8,128)(2,1)}, bf16[256,1536]{0,1:T(8,128)(2,1)}, u32[]{:S(2)}, u32[]{:S(2)}) %collective-permute-start.27) | collective-permute-done | bytes 786464 | tf_op jit(solution)/shard_map/ppermute | solution.py:128
  253.8 6.2 collective-permute-done.30
  274.0 9.2 %reshape.1496 = f32[4,2,128,1536]{2,1,0,3:T(2,128)} reshape(f32[1024,1536]{0,1:T(8,128)} %pad_maximum_fusion) | data formatting | bytes 12582912 | tf_op jit(solution)/shard_map/reshape | solution.py:210
  294.6 4.7 collective-permute-done.68
  310.1 6.8 %collective-permute-done.67 = bf16[128,1536]{0,1:T(8,128)(2,1)S(1)} collective-permute-done((bf16[128,1536]{0,1:T(8,128)(2,1)S(1)}, bf16[128,1536]{0,1:T(8,128)(2,1)S(1)}, u32[]{:S(2)}, u32[]{:S(2)}) %collective-permute-start.67) | collective-permute-done | bytes 393248 | tf_op jit(solution)/shard_map/ppermute | solution.py:128
  316.9 7.8 %collective-permute-done.69 = bf16[128,1536]{0,1:T(8,128)(2,1)S(1)} collective-permute-done((bf16[128,1536]{0,1:T(8,128)(2,1)S(1)}, bf16[128,1536]{0,1:T(8,128)(2,1)S(1)}, u32[]{:S(2)}, u32[]{:S(2)}) %collective-permute-start.69) | collective-permute-done | bytes 393248 | tf_op jit(solution)/shard_map/ppermute | solution.py:128
  331.3 11.0 %collective-permute-done.37 = bf16[256,1024]{1,0:T(8,128)(2,1)S(1)} collective-permute-done((bf16[256,1024]{1,0:T(8,128)(2,1)S(1)}, bf16[256,1024]{1,0:T(8,128)(2,1)S(1)}, u32[]{:S(2)}, u32[]{:S(2)}) %collective-permute-start.37) | collective-permute-done | bytes 524320 | tf_op jit(solution)/shard_map/ppermute | solution.py:124
  345.6 17.6 %collective-permute-done.39 = bf16[256,1024]{1,0:T(8,128)(2,1)S(1)} collective-permute-done((bf16[256,1024]{1,0:T(8,128)(2,1)S(1)}, bf16[256,1024]{1,0:T(8,128)(2,1)S(1)}, u32[]{:S(2)}, u32[]{:S(2)}) %collective-permute-start.39) | collective-permute-done | bytes 524320 | tf_op jit(solution)/shard_map/ppermute | solution.py:124
  385.7 9.8 %multiply_reduce_fusion.2 = (f32[6]{0:T(128)}, f32[1024,6]{0,1:T(8,128)}, f32[1024,6,64]{0,2,1:T(8,128)}) fusion(f32[1024,6,64]{0,2,1:T(8,128)S(1)} %get-tuple-element.286, f32[1024,6,64]{0,2,1:T(8,128)S(1)} %bitcast.563, f32[1024,6]{0,1:T(8,128)S(1)} %copy-done.94, f32[6]{0:T(128)S(1)} %copy-done.147, f32[6,1024]{1,0:T(8,128)S(1)} %bitcast.599, ...), kind=kOutput, calls=%fused_computation.76 | convolution fusion | flops 839903232 | bytes 10035248 | tf_op jit(solution)/shard_map/while/body/eval_jaxpr/hts,thp->shp/dot_general | solution.py:421
  395.6 17.3 %fusion.2 = (f32[6,1024]{1,0:T(8,128)S(1)}, f32[6,1024]{1,0:T(8,128)S(1)}, bf16[1024,1024]{1,0:T(8,128)(2,1)S(1)}) fusion(f32[6,1024]{1,0:T(8,128)S(1)} %bitcast.600, f32[1024,1024]{1,0:T(8,128)S(1)} %copy-done.34, pred[1024,1024]{1,0:T(8,128)(4,1)S(1)} %copy-done.47, f32[1024,6,64]{0,2,1:T(8,128)S(1)} %bitcast.564, f32[1024,6]{0,1:T(8,128)S(1)} %copy-done.94, ...), kind=kOutput, calls=%fused_computation.6 | convolution fusion | flops 874631168 | bytes 10584064 | tf_op jit(solution)/shard_map/while/body/eval_jaxpr/thp,shp->hts/dot_general | solution.py:424
  426.8 7.7 %fusion.162 = (f32[384]{0:T(512)}, f32[384]{0:T(512)}, f32[384]{0:T(512)}, f32[384]{0:T(512)}, f32[384]{0:T(512)}, /*index=5*/f32[1024,384]{1,0:T(8,128)S(1)}, bf16[1024,384]{1,0:T(8,128)(2,1)}) fusion(f32[1024,1408]{1,0:T(8,128)} %copy-done.1, f32[1023,384]{1,0:T(8,128)} %slice.734, pred[1024]{0:T(1024)(128)(4,1)S(1)} %copy-done.86, ...), kind=kLoop, calls=%fused_computation.431 | loop fusion | flops 12187776 | bytes 14943744 | tf_op jit(solution)/shard_map/while/body/eval_jaxpr/transpose(jvp())/reduce_sum | solution.py:53
  440.0 6.7 %fusion.35 = bf16[1024,64]{0,1:T(8,128)(2,1)} fusion(bf16[1024,2,64]{0,2,1:T(8,128)(2,1)S(1)} %bitcast.568, f32[1024,1024,2]{1,0,2:T(8,128)} %copy-done, f32[2,1024]{1,0:T(2,128)S(1)} %log_add_fusion, pred[1024,1024]{0,1:T(8,128)(4,1)S(1)} %copy-done.3), kind=kOutput, calls=%fused_computation.103 | convolution fusion | flops 276889600 | bytes 9838592 | tf_op jit(solution)/shard_map/while/body/eval_jaxpr/hts,thd->sd/dot_general | solution.py:462
  465.9 7.4 %reduce-window.29 = f32[6,8,128]{2,1,0:T(8,128)S(1)} reduce-window(f32[6,8,128]{2,1,0:T(8,128)S(1)} %bitcast.590, f32[]{:T(128)} %constant.293.clone.1), window={size=1x1x128 pad=0_0x0_0x0_127}, to_apply=%region_16.17 | reduce-window | flops 780288 | bytes 49156 | tf_op jit(solution)/shard_map/reduce-window.4
  488.9 5.2 concatenate.377
  494.1 6.3 fusion.178
  503.8 5.2 fusion.174
  518.7 15.2 %collective-permute-done.62 = bf16[128,512]{1,0:T(8,128)(2,1)S(1)} collective-permute-done((bf16[128,512]{1,0:T(8,128)(2,1)S(1)}, bf16[128,512]{1,0:T(8,128)(2,1)S(1)}, u32[]{:S(2)}, u32[]{:S(2)}) %collective-permute-start.62) | collective-permute-done | bytes 131104 | tf_op jit(solution)/shard_map/ppermute | solution.py:128
  547.0 5.8 collective-permute-done.51
  553.0 15.2 %collective-permute-done.53 = bf16[128,1408]{1,0:T(8,128)(2,1)} collective-permute-done((bf16[128,1408]{1,0:T(8,128)(2,1)}, bf16[128,1408]{1,0:T(8,128)(2,1)}, u32[]{:S(2)}, u32[]{:S(2)}) %collective-permute-start.53) | collective-permute-done | bytes 360480 | tf_op jit(solution)/shard_map/ppermute | solution.py:128
  (770 shorter events, 400.3 us)
Async XLA Ops:
  3.2 29.2 %collective-permute-start.1 = (bf16[48,512]{1,0:T(8,128)(2,1)S(1)}, bf16[48,512]{1,0:T(8,128)(2,1)}, u32[]{:S(2)}, u32[]{:S(2)}) collective-permute-start(bf16[48,512]{1,0:T(8,128)(2,1)S(1)} %pad_maximum_fusion.17), channel_id=1, source_target_pairs={{0,2},{1,3},{2,0},{3,1},{4,6},{5,7},{6,4},{7,5},{8,10},{9,11},{10,... | collective-permute-start | bytes 147464 | tf_op jit(solution)/shard_map/ppermute | solution.py:124
  6.2 26.4 %collective-permute-start = (bf16[48,512]{1,0:T(8,128)(2,1)S(1)}, bf16[48,512]{1,0:T(8,128)(2,1)}, u32[]{:S(2)}, u32[]{:S(2)}) collective-permute-start(bf16[48,512]{1,0:T(8,128)(2,1)S(1)} %pad_maximum_fusion.17), channel_id=1, source_target_pairs={{0,1},{1,0},{2,3},{3,2},{4,5},{5,4},{6,7},{7,6},{8,9},{9,8},{10,11... | collective-permute-start | bytes 147464 | tf_op jit(solution)/shard_map/ppermute | solution.py:124
  8.8 49.7 %collective-permute-start.16 = (bf16[128,512]{0,1:T(8,128)(2,1)}, bf16[128,512]{0,1:T(8,128)(2,1)}, u32[]{:S(2)}, u32[]{:S(2)}) collective-permute-start(bf16[128,512]{0,1:T(8,128)(2,1)} %get-tuple-element.324), channel_id=1, source_target_pairs={{0,4},{4,0},{8,12},{12,8},{16,20},{20,16},{24,28},{28,24},{1,5},{5... | collective-permute-start | bytes 393224 | tf_op jit(solution)/shard_map/ppermute | solution.py:124
  46.3 33.1 %collective-permute-start.11 = (bf16[128,1408]{1,0:T(8,128)(2,1)S(1)}, bf16[128,1408]{1,0:T(8,128)(2,1)S(1)}, u32[]{:S(2)}, u32[]{:S(2)}) collective-permute-start(bf16[128,1408]{1,0:T(8,128)(2,1)S(1)} %concatenate.351), channel_id=1, source_target_pairs={{0,4},{4,0},{8,12},{12,8},{16,20},{20,16},{24,28},{28,24},{1,5},{5... | collective-permute-start | bytes 1081352 | tf_op jit(solution)/shard_map/ppermute | solution.py:124
  57.0 32.5 %collective-permute-start.8 = (bf16[256,1024]{1,0:T(8,128)(2,1)}, bf16[256,1024]{1,0:T(8,128)(2,1)}, u32[]{:S(2)}, u32[]{:S(2)}) collective-permute-start(bf16[256,1024]{1,0:T(8,128)(2,1)} %multiply_convert_fusion.13), channel_id=1, source_target_pairs={{0,1},{1,0},{2,3},{3,2},{4,5},{5,4},{6,7},{7,6},{8,9},{9,8},{10,11... | collective-permute-start | bytes 1572872 | tf_op jit(solution)/shard_map/ppermute | solution.py:124
  83.0 32.0 %collective-permute-start.12 = (bf16[256,1408]{1,0:T(8,128)(2,1)S(1)}, bf16[256,1408]{1,0:T(8,128)(2,1)S(1)}, u32[]{:S(2)}, u32[]{:S(2)}) collective-permute-start(bf16[256,1408]{1,0:T(8,128)(2,1)S(1)} %pad_maximum_fusion.7), channel_id=1, source_target_pairs={{0,24},{4,28},{8,0},{12,4},{16,8},{20,12},{24,16},{28,20},{1,25},{... | collective-permute-start | bytes 2162696 | tf_op jit(solution)/shard_map/ppermute | solution.py:128
  101.3 26.1 %collective-permute-start.14 = (bf16[128,1408]{1,0:T(8,128)(2,1)S(1)}, bf16[128,1408]{1,0:T(8,128)(2,1)S(1)}, u32[]{:S(2)}, u32[]{:S(2)}) collective-permute-start(bf16[128,1408]{1,0:T(8,128)(2,1)S(1)} %slice.730), channel_id=1, source_target_pairs={{0,8},{4,12},{8,16},{12,20},{16,24},{20,28},{24,0},{28,4},{1,9},{5... | collective-permute-start | bytes 1081352 | tf_op jit(solution)/shard_map/ppermute | solution.py:128
  205.8 36.3 %collective-permute-start.27 = (bf16[256,1536]{0,1:T(8,128)(2,1)}, bf16[256,1536]{0,1:T(8,128)(2,1)}, u32[]{:S(2)}, u32[]{:S(2)}) collective-permute-start(bf16[256,1536]{0,1:T(8,128)(2,1)} %pad_maximum_fusion.6), channel_id=1, source_target_pairs={{0,24},{4,28},{8,0},{12,4},{16,8},{20,12},{24,16},{28,20},{1,25},{... | collective-permute-start | bytes 2359304 | tf_op jit(solution)/shard_map/ppermute | solution.py:128
  217.6 28.9 %collective-permute-start.22 = (bf16[256,1024]{1,0:T(8,128)(2,1)}, bf16[256,1024]{1,0:T(8,128)(2,1)}, u32[]{:S(2)}, u32[]{:S(2)}) collective-permute-start(bf16[256,1024]{1,0:T(8,128)(2,1)} %fusion.86), channel_id=1, source_target_pairs={{0,2},{1,3},{2,0},{3,1},{4,6},{5,7},{6,4},{7,5},{8,10},{9,11},{10,... | collective-permute-start | bytes 1572872 | tf_op jit(solution)/shard_map/ppermute | solution.py:124
  229.4 24.2 %collective-permute-start.29 = (bf16[128,1536]{0,1:T(8,128)(2,1)S(1)}, bf16[128,1536]{0,1:T(8,128)(2,1)S(1)}, u32[]{:S(2)}, u32[]{:S(2)}) collective-permute-start(bf16[128,1536]{0,1:T(8,128)(2,1)S(1)} %slice.767), channel_id=1, source_target_pairs={{0,8},{4,12},{8,16},{12,20},{16,24},{20,28},{24,0},{28,4},{1,9},{5... | collective-permute-start | bytes 1179656 | tf_op jit(solution)/shard_map/ppermute | solution.py:128
  292.5 34.2 %collective-permute-start.36 = (bf16[2,256,1024]{2,1,0:T(8,128)(2,1)S(1)}, bf16[2,256,1024]{2,1,0:T(8,128)(2,1)S(1)}, u32[]{:S(2)}, u32[]{:S(2)}) collective-permute-start(bf16[2,256,1024]{2,1,0:T(8,128)(2,1)S(1)} %fusion.40), channel_id=1, source_target_pairs={{0,1},{1,0},{2,3},{3,2},{4,5},{5,4},{6,7},{7,6},{8,9},{9,8},{10,11... | collective-permute-start | bytes 3145736 | tf_op jit(solution)/shard_map/ppermute | solution.py:124
  299.4 25.3 %collective-permute-start.69 = (bf16[128,1536]{0,1:T(8,128)(2,1)S(1)}, bf16[128,1536]{0,1:T(8,128)(2,1)S(1)}, u32[]{:S(2)}, u32[]{:S(2)}) collective-permute-start(bf16[128,1536]{0,1:T(8,128)(2,1)S(1)} %fusion.61), channel_id=1, source_target_pairs={{0,24},{4,28},{8,0},{12,4},{16,8},{20,12},{24,16},{28,20},{1,25},{... | collective-permute-start | bytes 1179656 | tf_op jit(solution)/shard_map/ppermute | solution.py:128
  304.0 25.0 %collective-permute-start.31 = (bf16[2,256,1024]{2,1,0:T(8,128)(2,1)S(1)}, bf16[2,256,1024]{2,1,0:T(8,128)(2,1)S(1)}, u32[]{:S(2)}, u32[]{:S(2)}) collective-permute-start(bf16[2,256,1024]{2,1,0:T(8,128)(2,1)S(1)} %fusion.39), channel_id=1, source_target_pairs={{0,1},{1,0},{2,3},{3,2},{4,5},{5,4},{6,7},{7,6},{8,9},{9,8},{10,11... | collective-permute-start | bytes 3145736 | tf_op jit(solution)/shard_map/ppermute | solution.py:124
  308.6 36.8 %collective-permute-start.66 = (bf16[128,1536]{0,1:T(8,128)(2,1)S(1)}, bf16[128,1536]{0,1:T(8,128)(2,1)S(1)}, u32[]{:S(2)}, u32[]{:S(2)}) collective-permute-start(bf16[128,1536]{0,1:T(8,128)(2,1)S(1)} %get-tuple-element.291), channel_id=1, source_target_pairs={{0,24},{4,28},{8,0},{12,4},{16,8},{20,12},{24,16},{28,20},{1,25},{... | collective-permute-start | bytes 1179656 | tf_op jit(solution)/shard_map/ppermute | solution.py:128
  330.8 263.6 %collective-permute-start.32 = (bf16[256,1024]{1,0:T(8,128)(2,1)}, bf16[256,1024]{1,0:T(8,128)(2,1)}, u32[]{:S(2)}, u32[]{:S(2)}) collective-permute-start(bf16[256,1024]{1,0:T(8,128)(2,1)} %fusion.87), channel_id=1, source_target_pairs={{0,2},{1,3},{2,0},{3,1},{4,6},{5,7},{6,4},{7,5},{8,10},{9,11},{10,... | collective-permute-start | bytes 1572872 | tf_op jit(solution)/shard_map/ppermute | solution.py:124
  460.3 51.7 %collective-permute-start.57 = (bf16[128,512]{1,0:T(8,128)(2,1)}, bf16[128,512]{1,0:T(8,128)(2,1)}, u32[]{:S(2)}, u32[]{:S(2)}) collective-permute-start(bf16[128,512]{1,0:T(8,128)(2,1)} %get-tuple-element.299), channel_id=1, source_target_pairs={{0,8},{4,12},{8,16},{12,20},{16,24},{20,28},{24,0},{28,4},{1,9},{5... | collective-permute-start | bytes 393224 | tf_op jit(solution)/shard_map/ppermute | solution.py:128
  460.6 54.7 %collective-permute-start.61 = (bf16[128,512]{1,0:T(8,128)(2,1)}, bf16[128,512]{1,0:T(8,128)(2,1)}, u32[]{:S(2)}, u32[]{:S(2)}) collective-permute-start(bf16[128,512]{1,0:T(8,128)(2,1)} %get-tuple-element.300), channel_id=1, source_target_pairs={{0,24},{4,28},{8,0},{12,4},{16,8},{20,12},{24,16},{28,20},{1,25},{... | collective-permute-start | bytes 393224 | tf_op jit(solution)/shard_map/ppermute | solution.py:128
  464.1 54.5 %collective-permute-start.60 = (bf16[128,512]{1,0:T(8,128)(2,1)}, bf16[128,512]{1,0:T(8,128)(2,1)}, u32[]{:S(2)}, u32[]{:S(2)}) collective-permute-start(bf16[128,512]{1,0:T(8,128)(2,1)} %get-tuple-element.301), channel_id=1, source_target_pairs={{0,8},{4,12},{8,16},{12,20},{16,24},{20,28},{24,0},{28,4},{1,9},{5... | collective-permute-start | bytes 393224 | tf_op jit(solution)/shard_map/ppermute | solution.py:128
  511.4 23.5 %collective-permute-start.48 = (bf16[128,1408]{1,0:T(8,128)(2,1)}, bf16[128,1408]{1,0:T(8,128)(2,1)S(1)}, u32[]{:S(2)}, u32[]{:S(2)}) collective-permute-start(bf16[128,1408]{1,0:T(8,128)(2,1)} %get-tuple-element.293), channel_id=1, source_target_pairs={{0,8},{4,12},{8,16},{12,20},{16,24},{20,28},{24,0},{28,4},{1,9},{5... | collective-permute-start | bytes 1081352 | tf_op jit(solution)/shard_map/ppermute | solution.py:128
  512.0 24.1 %collective-permute-start.52 = (bf16[128,1408]{1,0:T(8,128)(2,1)S(1)}, bf16[128,1408]{1,0:T(8,128)(2,1)S(1)}, u32[]{:S(2)}, u32[]{:S(2)}) collective-permute-start(bf16[128,1408]{1,0:T(8,128)(2,1)S(1)} %get-tuple-element.294), channel_id=1, source_target_pairs={{0,24},{4,28},{8,0},{12,4},{16,8},{20,12},{24,16},{28,20},{1,25},{... | collective-permute-start | bytes 1081352 | tf_op jit(solution)/shard_map/ppermute | solution.py:128
  533.8 37.0 %collective-permute-start.41 = (bf16[2,256,1024]{2,1,0:T(8,128)(2,1)S(1)}, bf16[2,256,1024]{2,1,0:T(8,128)(2,1)}, u32[]{:S(2)}, u32[]{:S(2)}) collective-permute-start(bf16[2,256,1024]{2,1,0:T(8,128)(2,1)S(1)} %fusion.41), channel_id=1, source_target_pairs={{0,1},{1,0},{2,3},{3,2},{4,5},{5,4},{6,7},{7,6},{8,9},{9,8},{10,11... | collective-permute-start | bytes 3145736 | tf_op jit(solution)/shard_map/ppermute | solution.py:124
  542.6 33.9 %collective-permute-start.50 = (bf16[128,1408]{1,0:T(8,128)(2,1)}, bf16[128,1408]{1,0:T(8,128)(2,1)S(1)}, u32[]{:S(2)}, u32[]{:S(2)}) collective-permute-start(bf16[128,1408]{1,0:T(8,128)(2,1)} %get-tuple-element.296), channel_id=1, source_target_pairs={{0,24},{4,28},{8,0},{12,4},{16,8},{20,12},{24,16},{28,20},{1,25},{... | collective-permute-start | bytes 1081352 | tf_op jit(solution)/shard_map/ppermute | solution.py:128
  543.8 24.4 %collective-permute-start.53 = (bf16[128,1408]{1,0:T(8,128)(2,1)}, bf16[128,1408]{1,0:T(8,128)(2,1)}, u32[]{:S(2)}, u32[]{:S(2)}) collective-permute-start(bf16[128,1408]{1,0:T(8,128)(2,1)} %get-tuple-element.282), channel_id=1, source_target_pairs={{0,24},{4,28},{8,0},{12,4},{16,8},{20,12},{24,16},{28,20},{1,25},{... | collective-permute-start | bytes 1081352 | tf_op jit(solution)/shard_map/ppermute | solution.py:128
  552.7 23.8 %collective-permute-start.49 = (bf16[128,1408]{1,0:T(8,128)(2,1)}, bf16[128,1408]{1,0:T(8,128)(2,1)S(1)}, u32[]{:S(2)}, u32[]{:S(2)}) collective-permute-start(bf16[128,1408]{1,0:T(8,128)(2,1)} %get-tuple-element.281), channel_id=1, source_target_pairs={{0,8},{4,12},{8,16},{12,20},{16,24},{20,28},{24,0},{28,4},{1,9},{5... | collective-permute-start | bytes 1081352 | tf_op jit(solution)/shard_map/ppermute | solution.py:128
  (212 other events, 2526.2 us)

commit v2 on v1

v2 whole, which is shorter than its diff:
```python
import functools

import jax
import jax.numpy as jnp
from jax import lax
from jax.experimental import pallas as pl
from jax.experimental.pallas import tpu as pltpu
from jax.sharding import PartitionSpec as P

STATE = 128
CONV = 4
HEADS = 8
KV_HEADS = 2
HEAD = 64

EPS = 1e-06
ROPE_BASE = 10000.0
NEG_FILL = -1e30


def contract_rows(left_side, right_side):
    return lax.dot_general(
        left_side, right_side, (((0,), (0,)), ((), ())), preferred_element_type=jnp.float32
    )


def contract_cols(left_side, right_side):
    return lax.dot_general(
        left_side, right_side, (((1,), (1,)), ((), ())), preferred_element_type=jnp.float32
    )


def split_cols(matrix, widths):
    pieces = []
    begin_at = 0
    for part_width in widths:
        pieces.append(matrix[:, begin_at : begin_at + part_width])
        begin_at = begin_at + part_width
    return pieces


def flip(values, axis, mask):
    size = lax.axis_size(axis)
    return lax.ppermute(values, axis, [(i, i ^ mask) for i in range(size)])


def ring(values, step):
    return lax.ppermute(values, "fsdp", [(i, (i + 2 * step) % 8) for i in range(8)])


def staged():
    return lax.axis_size("fsdp") == 8


def place_bits():
    index = lax.axis_index("tp")
    return index // 2, index % 2


def gather_pieces(rows_in):
    far = flip(rows_in, "tp", 2)
    near = flip(rows_in, "tp", 1)
    cross = flip(far, "tp", 1)
    return rows_in, far, near, cross


def reduce_pieces(keep, give):
    half = keep.shape[0] // 2
    near = flip(give, "tp", 1)
    passed = (keep[half:] + near[half:].astype(jnp.float32)).astype(jnp.bfloat16)
    far = flip(passed, "tp", 2)
    return keep, near, far


def fsdp_place():
    index = lax.axis_index("fsdp")
    return index // 2, index % 2


class Scatter:
    def __init__(self, grads):
        self.grads = grads
        self.rows = grads[0].shape[0] // 8
        self.carried = None
        if staged():
            self.came = self.exchange(3)

    def part(self, dy, dz):
        rows = slice((dy * 4 + dz) * self.rows, (dy * 4 + dz + 1) * self.rows)
        if len(self.grads) == 1:
            return self.grads[0][rows]
        return jnp.concatenate([grad[rows] for grad in self.grads], axis=1)

    def exchange(self, dz):
        return flip(self.part(1, dz), "fsdp", 1)

    def summed(self, dz):
        total = self.part(0, dz).astype(jnp.float32) + self.came.astype(jnp.float32)
        return total if self.carried is None else total + self.carried.astype(jnp.float32)

    def step(self, dz):
        if not staged():
            return ()
        self.carried = ring(self.summed(dz).astype(jnp.bfloat16), 1)
        self.came = self.exchange(dz - 1)
        return self.carried, self.came

    def total(self):
        if not staged():
            return lax.psum_scatter(
                jnp.concatenate(self.grads, axis=1), "fsdp", scatter_dimension=0, tiled=True
            ).astype(jnp.float32)
        return self.summed(0)


class Gather:
    def __init__(self, shard):
        self.shard = shard
        if staged():
            self.along, self.across = [shard], [flip(shard, "fsdp", 1)]

    def step(self):
        if not staged():
            return ()
        came = ring(self.along[-1], 1)
        self.along.append(came)
        self.across.append(flip(came, "fsdp", 1))
        return came, self.across[-1]

    def parts(self):
        if not staged():
            return [lax.all_gather(self.shard, "fsdp", axis=0, tiled=True)]
        return [blocks[-dz % 4] for blocks in (self.along, self.across) for dz in range(4)]


def sum_fsdp(values):
    if not staged():
        return lax.psum(values, "fsdp")
    for mask in (1, 2, 6):
        values = values + flip(values, "fsdp", mask)
    return values


def sum_tp(values):
    for mask in (1, 2):
        values = values + flip(values, "tp", mask)
    return values


def feature_order():
    if not staged():
        return jnp.arange(8, dtype=jnp.int32)
    z_at, y_at = fsdp_place()
    steps = jnp.arange(8, dtype=jnp.int32)
    return (z_at + steps % 4) % 4 * 2 + (y_at ^ (steps // 4))


CHUNK = 32


def row_chunks(rows, body, carry=0):
    def step(k, carry):
        return body(pl.ds(pl.multiple_of(k * CHUNK, CHUNK), CHUNK), carry)

    return lax.fori_loop(0, rows // CHUNK, step, carry)


def front_body(order_ref, tok_ref, cot_ref, both_ref, tok_rel):
    rows_all, width = tok_ref.shape
    block = width // 8

    def chunk(rows, carry):
        below = pl.ds(pl.multiple_of(rows.start + rows_all, CHUNK), CHUNK)
        for b in range(8):
            there = pl.ds(pl.multiple_of(order_ref[b] * block, block), block)
            here = slice(b * block, b * block + block)
            tok_rel[rows, here] = tok_ref[rows, there]
            both_ref[below, here] = cot_ref[rows, there]
        values = tok_rel[rows].astype(jnp.float32)
        normed = values * lax.rsqrt(jnp.mean(values * values, axis=-1, keepdims=True) + EPS)
        both_ref[rows] = normed.astype(jnp.bfloat16)
        return carry

    row_chunks(rows_all, chunk)


def summed_rows(rows, keep_ref, near_ref, far_ref):
    return (
        keep_ref[rows] + near_ref[rows].astype(jnp.float32) + far_ref[rows].astype(jnp.float32)
    )


def mixed_body(_, tok_ref, keep_ref, near_ref, far_ref, gain_ref, after_ref, second_ref):
    def chunk(rows, carry):
        after = tok_ref[rows].astype(jnp.float32) + summed_rows(rows, keep_ref, near_ref, far_ref)
        after_ref[rows] = after
        normed = after * lax.rsqrt(jnp.mean(after * after, axis=-1, keepdims=True) + EPS)
        second_ref[rows] = (normed * gain_ref[...]).astype(jnp.bfloat16)
        return carry

    row_chunks(tok_ref.shape[0], chunk)


def output_body(order_ref, after_ref, keep_ref, near_ref, far_ref, out_ref):
    block = after_ref.shape[1] // 8

    def chunk(rows, carry):
        values = after_ref[rows] + summed_rows(rows, keep_ref, near_ref, far_ref)
        values = values.astype(jnp.bfloat16)
        for b in range(8):
            there = pl.ds(pl.multiple_of(order_ref[b] * block, block), block)
            out_ref[rows, there] = values[:, b * block : b * block + block]
        return carry

    row_chunks(after_ref.shape[0], chunk)


def norm_back(values, d_out, gain):
    inverse = lax.rsqrt(jnp.mean(values * values, axis=-1, keepdims=True) + EPS)
    normed = values * inverse
    scaled = d_out * gain
    return inverse * (scaled - normed * jnp.mean(scaled * normed, axis=-1, keepdims=True))


def after_back_body(
    _, after_ref, cot_ref, keep_ref, near_ref, far_ref, gain_ref, d_after_ref, d_mix_ref
):
    def chunk(rows, carry):
        d_second = summed_rows(rows, keep_ref, near_ref, far_ref)
        lower = pl.ds(pl.multiple_of(rows.start + after_ref.shape[0], CHUNK), CHUNK)
        d_after = cot_ref[lower].astype(jnp.float32) + norm_back(
            after_ref[rows], d_second, gain_ref[...]
        )
        d_after_ref[rows] = d_after
        d_mix_ref[rows] = d_after.astype(jnp.bfloat16)
        return carry

    row_chunks(after_ref.shape[0], chunk)


def token_back_body(
    order_ref, tok_ref, d_after_ref, keep_ref, near_ref, far_ref, gain_ref, out_ref
):
    block = tok_ref.shape[1] // 8

    def chunk(rows, carry):
        d_first = summed_rows(rows, keep_ref, near_ref, far_ref)
        values = d_after_ref[rows] + norm_back(
            tok_ref[rows].astype(jnp.float32), d_first, gain_ref[...]
        )
        for b in range(8):
            there = pl.ds(pl.multiple_of(order_ref[b] * block, block), block)
            out_ref[rows, there] = values[:, b * block : b * block + block]
        return carry

    row_chunks(tok_ref.shape[0], chunk)


def piece_at(block, at):
    apart = block ^ at
    return (apart & 1) * 2 + (apart >> 1)


def head_lanes(columns, first, lanes):
    rows = columns.shape[0]
    even = jnp.broadcast_to(columns[:, first : first + 1], (rows, 128))
    odd = jnp.broadcast_to(columns[:, first + 1 : first + 2], (rows, 128))
    return jnp.where(lanes < HEAD, even, odd)


def lane_ids(rows, cols):
    return lax.broadcasted_iota(jnp.int32, (rows, cols), 1)


def row_ids(rows, cols):
    return lax.broadcasted_iota(jnp.int32, (rows, cols), 0)


def dot_nt(left_side, right_side, **kw):
    return lax.dot_general(
        left_side, right_side, (((1,), (1,)), ((), ())), preferred_element_type=jnp.float32, **kw
    )


def dot_nn(left_side, right_side):
    return jnp.dot(left_side, right_side, preferred_element_type=jnp.float32)


def dot_tn(left_side, right_side):
    return lax.dot_general(
        left_side, right_side, (((0,), (0,)), ((), ())), preferred_element_type=jnp.float32
    )


def conv_window(window, taps, offset, keep):
    rows = window.shape[0] - 8
    summed = window[8:] * taps[CONV - 1 : CONV] + offset
    for lag in range(1, CONV):
        summed = summed + window[8 - lag : 8 - lag + rows] * keep[:, lag : lag + 1] * (
            taps[CONV - 1 - lag : CONV - lag]
        )
    return summed


def log_one_plus(values):
    ratio = values / (2.0 + values)
    square = ratio * ratio
    series = jnp.full_like(values, 1.0 / 15.0)
    for odd in (13, 11, 9, 7, 5, 3, 1):
        series = series * square + 1.0 / odd
    return 2.0 * ratio * series


def scan_lanes(values, reverse):
    length = values.shape[1]
    lanes = lane_ids(*values.shape)
    step = 1
    while step < length:
        if reverse:
            moved = jnp.where(lanes < length - step, pltpu.roll(values, length - step, 1), 0.0)
        else:
            moved = jnp.where(lanes >= step, pltpu.roll(values, step, 1), 0.0)
        values = values + moved
        step = step * 2
    return values


def pair_mask(seg_col, seg_row, at_t, at_s):
    size = seg_col.shape[0]
    rows = row_ids(size, size) + at_t * size
    cols = lane_ids(size, size) + at_s * size
    return (seg_col == seg_row) & (rows >= cols)


def swap_halves(values, lanes):
    half = HEAD // 2
    return jnp.where(
        lanes % HEAD < half, pltpu.roll(values, 128 - half, 1), pltpu.roll(values, half, 1)
    )


def ssd_forward_body(
    heads,
    at_ref,
    proj_ref,
    segc_ref,
    segr_ref,
    keep_ref,
    taps_ref,
    tapb_ref,
    rate_ref,
    scan_ref,
    xpre_ref,
    bpre_ref,
    basis_ref,
    inputs_ref,
    rows_ref,
    cols_ref,
    xpad,
    bpad,
    dtr,
):
    blocks, size = proj_ref.shape[0], proj_ref.shape[1]
    channels = xpre_ref.shape[1]
    states = bpre_ref.shape[1]
    tail = proj_ref.shape[2] - states - 128
    at = at_ref[0]
    xpad[0:8] = jnp.zeros((8, channels), jnp.float32)
    bpad[0:8] = jnp.zeros((8, states), jnp.float32)

    def load(a, carry):
        rows = pl.ds(pl.multiple_of(a * size + 8, 8), size)
        block = piece_at(a, at)
        xpad[rows] = proj_ref[block, :, :channels]
        bpad[rows] = proj_ref[block, :, tail : tail + states]
        steps = proj_ref[block, :, tail + states :]
        dtr[:, pl.ds(pl.multiple_of(a * size, size), size)] = steps.T[0:8]
        return carry

    lax.fori_loop(0, blocks, load, 0)
    raw = dtr[...] + rate_ref[:, 0:1]
    step_size = jnp.maximum(raw, 0.0) + log_one_plus(jnp.exp(-jnp.abs(raw)))
    log_rate = -step_size * jnp.exp(rate_ref[:, 1:2])
    cum = scan_lanes(log_rate, False)
    length = raw.shape[1]
    rows_ref[0:8] = step_size
    rows_ref[8:16] = cum
    rows_ref[16:24] = raw
    cols_ref[...] = jnp.concatenate(
        [step_size, cum, jnp.zeros((112, length), jnp.float32)], axis=0
    ).T
    lanes = lane_ids(size, 128)

    def prepare_block(a, carry):
        window = pl.ds(pl.multiple_of(a * size, size), size + 8)
        rows = pl.ds(pl.multiple_of(a * size, size), size)
        keep = keep_ref[rows]
        columns = cols_ref[rows]
        bpre = conv_window(bpad[window], tapb_ref[0:4], tapb_ref[4:5], keep)
        bpre_ref[rows] = bpre
        basis_ref[rows] = (bpre * jax.nn.sigmoid(bpre)).astype(jnp.bfloat16)
        for pair in range(channels // 128):
            span = slice(pair * 128, pair * 128 + 128)
            xpre = conv_window(xpad[window, span], taps_ref[0:4, span], taps_ref[4:5, span], keep)
            xpre_ref[rows, span] = xpre
            mixed = (xpre * jax.nn.sigmoid(xpre)).astype(jnp.bfloat16).astype(jnp.float32)
            steps = head_lanes(columns, 2 * pair, lanes)
            inputs_ref[rows, span] = (steps * mixed).astype(jnp.bfloat16)
        return carry

    lax.fori_loop(0, blocks, prepare_block, 0)
    state = states // 2

    def row_block(i, carry):
        rows_t = pl.ds(pl.multiple_of(i * size, size), size)
        basis_c = basis_ref[rows_t, state:]
        seg_t = segc_ref[rows_t]
        columns = cols_ref[rows_t]

        def pair_block(j, totals):
            rows_s = pl.ds(pl.multiple_of(j * size, size), size)
            allowed = pair_mask(seg_t, segr_ref[:, rows_s], i, j)
            gram = jnp.where(allowed, dot_nt(basis_c, basis_ref[rows_s, :state]), 0.0)
            cum_s = rows_ref[8:16, rows_s]
            fresh = []
            for pair in range(heads // 2):
                values = inputs_ref[rows_s, pair * 128 : pair * 128 + 128]
                outs = []
                for h in (2 * pair, 2 * pair + 1):
                    spread = columns[:, 8 + h : 9 + h] - cum_s[h : h + 1]
                    weights = (gram * jnp.exp(jnp.minimum(spread, 0.0))).astype(jnp.bfloat16)
                    outs.append(dot_nn(weights, values))
                fresh.append(totals[pair] + jnp.where(lanes < HEAD, outs[0], outs[1]))
            return tuple(fresh)

        zero = jnp.zeros((size, 128), jnp.float32)
        totals = lax.fori_loop(0, i + 1, pair_block, (zero,) * (heads // 2))
        for pair in range(heads // 2):
            scan_ref[rows_t, pair * 128 : pair * 128 + 128] = totals[pair]
        return carry

    lax.fori_loop(0, blocks, row_block, 0)


def attend_forward_body(
    count,
    at_ref,
    first_ref,
    proj_ref,
    scan_ref,
    xpre_ref,
    segc_ref,
    segr_ref,
    cos_ref,
    sin_ref,
    gain_ref,
    *refs,
):
    parts = refs[:count]
    cat_ref, gate_ref, query_ref, keyk_ref, valv_ref, logs_ref, inv_ref, weight_ref = refs[count:]
    stack_rows(parts, weight_ref)
    blocks, size = proj_ref.shape[0], proj_ref.shape[1]
    channels = scan_ref.shape[1]
    at = at_ref[0]
    lanes = lane_ids(size, 128)
    half_type = jnp.bfloat16

    def finish_block(a, carry):
        rows = pl.ds(pl.multiple_of(a * size, size), size)
        block = piece_at(a, at)
        xpre = xpre_ref[rows]
        mixed = (xpre * jax.nn.sigmoid(xpre)).astype(half_type).astype(jnp.float32)
        mine = dot_nn(first_ref[block], weight_ref[:, : channels + 128])
        gate, query = mine[:, :channels], mine[:, channels:]
        gate_ref[block] = gate
        gated = (scan_ref[rows] + gain_ref[1:2] * mixed) * (gate * jax.nn.sigmoid(gate))
        inverse = lax.rsqrt(jnp.mean(gated * gated, axis=-1, keepdims=True) + EPS)
        inv_ref[rows] = jnp.broadcast_to(inverse, (size, 128))
        cat_ref[block, :, :channels] = (gated * inverse * gain_ref[0:1]).astype(half_type)
        cosine, sine = cos_ref[rows], sin_ref[rows]
        query_ref[rows] = (query * cosine + swap_halves(query, lanes) * sine).astype(half_type)
        keyval = proj_ref[block, :, channels : channels + 128]
        keyval = keyval * jnp.where(lanes < HEAD, cosine, 1.0) + swap_halves(
            keyval, lanes
        ) * jnp.where(lanes < HEAD, sine, 0.0)
        moved = pltpu.roll(keyval, HEAD, 1)
        keyk_ref[rows] = jnp.where(lanes < HEAD, keyval, moved).astype(half_type)
        valv_ref[rows] = jnp.where(lanes < HEAD, moved, keyval).astype(half_type)
        return carry

    lax.fori_loop(0, blocks, finish_block, 0)
    for i in range(blocks):
        width = (i + 1) * size
        rows = slice(i * size, width)
        query = query_ref[rows]
        places = row_ids(size, width) + i * size
        allowed = (segc_ref[rows] == segr_ref[:, :width]) & (places >= lane_ids(size, width))
        outs, logs = [], []
        for h in range(2):
            mine = (lanes < HEAD) if h == 0 else (lanes >= HEAD)
            masked = jnp.where(mine, query, jnp.zeros_like(query))
            scores = dot_nt(masked, keyk_ref[:width]) * HEAD ** (-0.5)
            scores = jnp.where(allowed, scores, NEG_FILL)
            top = jnp.max(scores, axis=-1, keepdims=True)
            powers = jnp.exp(scores - top)
            total = jnp.sum(powers, axis=-1, keepdims=True)
            outs.append(dot_nn(powers.astype(half_type), valv_ref[:width]) / total)
            logs.append(top + jnp.log(total))
        cat_ref[piece_at(i, at), :, channels:] = jnp.where(lanes < HEAD, outs[0], outs[1]).astype(half_type)
        logs_ref[rows] = jnp.where(lanes < HEAD, logs[0], logs[1])


def attend_backward_body(
    at_ref,
    gate_ref,
    mine_ref,
    far_ref,
    near_ref,
    cross_ref,
    weight_ref,
    scan_ref,
    xpre_ref,
    segc_ref,
    segr_ref,
    cos_ref,
    sin_ref,
    gain_ref,
    query_ref,
    keyk_ref,
    valv_ref,
    logs_ref,
    inv_ref,
    dproj_ref,
    dcomb_ref,
    small_ref,
    dmix_ref,
    dkey,
    dval,
    dcat_ref,
):
    wide = dcat_ref.shape[2]
    for p, piece in enumerate((mine_ref, far_ref, near_ref, cross_ref)):
        dmix_ref[p] = piece[...]
        dcat_ref[p] = dot_nn(piece[...], weight_ref[:, weight_ref.shape[1] - wide :])
    blocks, size = gate_ref.shape[0], gate_ref.shape[1]
    channels = scan_ref.shape[1]
    at = at_ref[0]
    lanes = lane_ids(size, 128)
    half_type = jnp.bfloat16

    def finish_block(a, carry):
        grad_gain, grad_skip = carry
        rows = pl.ds(pl.multiple_of(a * size, size), size)
        block = piece_at(a, at)
        xpre = xpre_ref[rows]
        mixed = (xpre * jax.nn.sigmoid(xpre)).astype(half_type).astype(jnp.float32)
        gate = gate_ref[block]
        sig = jax.nn.sigmoid(gate)
        act = gate * sig
        combined = scan_ref[rows] + gain_ref[1:2] * mixed
        inverse = inv_ref[rows, 0:1]
        normed = combined * act * inverse
        d_out = dcat_ref[block, :, :channels]
        grad_gain = grad_gain + jnp.sum(d_out * normed, axis=0, keepdims=True)
        scaled = d_out * gain_ref[0:1]
        d_gated = inverse * (scaled - normed * jnp.mean(scaled * normed, axis=-1, keepdims=True))
        d_comb = d_gated * act
        dcomb_ref[rows] = d_comb
        grad_skip = grad_skip + jnp.sum(d_comb * mixed, axis=0, keepdims=True)
        d_gate = d_gated * combined * sig * (1.0 + gate * (1.0 - sig))
        dproj_ref[block, :, :channels] = d_gate.astype(half_type)
        return grad_gain, grad_skip

    zero = jnp.zeros((1, channels), jnp.float32)
    grad_gain, grad_skip = lax.fori_loop(0, blocks, finish_block, (zero, zero))
    small_ref[...] = jnp.concatenate(
        [grad_gain, grad_skip, jnp.zeros((6, channels), jnp.float32)], axis=0
    )
    dkey[...] = jnp.zeros_like(dkey)
    dval[...] = jnp.zeros_like(dval)
    for i in range(blocks):
        width = (i + 1) * size
        rows = slice(i * size, width)
        query = query_ref[rows]
        d_att = dcat_ref[piece_at(i, at), :, channels:].astype(half_type)
        logs = logs_ref[rows]
        places = row_ids(size, width) + i * size
        allowed = (segc_ref[rows] == segr_ref[:, :width]) & (places >= lane_ids(size, width))
        outs = []
        for h in range(2):
            mine = (lanes < HEAD) if h == 0 else (lanes >= HEAD)
            masked = jnp.where(mine, query, jnp.zeros_like(query))
            d_masked = jnp.where(mine, d_att, jnp.zeros_like(d_att))
            scores = dot_nt(masked, keyk_ref[:width]) * HEAD ** (-0.5)
            scores = jnp.where(allowed, scores, NEG_FILL)
            probs = jnp.exp(scores - logs[:, h * HEAD : h * HEAD + 1])
            d_probs = dot_nt(d_masked, valv_ref[:width])
            mean = jnp.sum(probs * d_probs, axis=-1, keepdims=True)
            d_scores = (probs * (d_probs - mean)).astype(half_type)
            outs.append(dot_nn(d_scores, keyk_ref[:width]))
            dkey[:width] += dot_tn(d_scores, masked)
            dval[:width] += dot_tn(probs.astype(half_type), d_masked)
        d_query = jnp.where(lanes < HEAD, outs[0], outs[1]) * HEAD ** (-0.5)
        cosine, sine = cos_ref[rows], sin_ref[rows]
        d_query = d_query * cosine - swap_halves(d_query, lanes) * sine
        dproj_ref[piece_at(i, at), :, channels : channels + 128] = d_query.astype(half_type)

    def key_block(a, carry):
        rows = pl.ds(pl.multiple_of(a * size, size), size)
        d_key, d_val = dkey[rows], dval[rows]
        d_key = (d_key + pltpu.roll(d_key, HEAD, 1)) * HEAD ** (-0.5)
        d_val = d_val + pltpu.roll(d_val, HEAD, 1)
        d_key = d_key * cos_ref[rows] - swap_halves(d_key, lanes) * sin_ref[rows]
        dproj_ref[piece_at(a, at), :, channels + 128 :] = jnp.where(lanes < HEAD, d_key, d_val).astype(
            half_type
        )
        return carry

    lax.fori_loop(0, blocks, key_block, 0)


def silu_slope(values):
    sig = jax.nn.sigmoid(values)
    return sig * (1.0 + values * (1.0 - sig))


def conv_back(d_window, keep_window, taps):
    rows = d_window.shape[0] - 8
    summed = d_window[:rows] * taps[CONV - 1 : CONV]
    for lag in range(1, CONV):
        moved = d_window * keep_window[:, lag : lag + 1]
        summed = summed + moved[lag : lag + rows] * taps[CONV - 1 - lag : CONV - lag]
    return summed


def conv_grads(d_pre, window, keep):
    rows = d_pre.shape[0]
    sums = []
    for tap in range(CONV):
        lag = CONV - 1 - tap
        moved = window[8 - lag : 8 - lag + rows]
        if lag:
            moved = moved * keep[:, lag : lag + 1]
        sums.append(jnp.sum(d_pre * moved, axis=0, keepdims=True))
    sums.append(jnp.sum(d_pre, axis=0, keepdims=True))
    sums.append(jnp.zeros((8 - len(sums), d_pre.shape[1]), jnp.float32))
    return jnp.concatenate(sums, axis=0)


def ssd_backward_body(
    heads,
    at_ref,
    proj_ref,
    dcomb_ref,
    scan_ref,
    segc_ref,
    segr_ref,
    keep_ref,
    taps_ref,
    tapb_ref,
    rate_ref,
    gain_ref,
    xpre_ref,
    bpre_ref,
    basis_ref,
    inputs_ref,
    rows_ref,
    cols_ref,
    dproj_ref,
    gradx_ref,
    gradb_ref,
    grads_ref,
    xpad,
    bpad,
    dpx,
    dpb,
    dsc,
    dst,
    cbt,
    mixt,
    dint,
    dbt,
    dcb,
    qrow,
):
    blocks, size = proj_ref.shape[0], proj_ref.shape[1]
    channels = xpre_ref.shape[1]
    states = bpre_ref.shape[1]
    state = states // 2
    tail = proj_ref.shape[2] - states - 128
    length = blocks * size
    at = at_ref[0]
    half_type = jnp.bfloat16
    lanes = lane_ids(size, 128)
    xpad[0:8] = jnp.zeros((8, channels), jnp.float32)
    bpad[0:8] = jnp.zeros((8, states), jnp.float32)
    dpx[length : length + 8] = jnp.zeros((8, channels), jnp.float32)
    dpb[length : length + 8] = jnp.zeros((8, states), jnp.float32)
    dint[...] = jnp.zeros_like(dint)
    dbt[...] = jnp.zeros_like(dbt)
    head_of = jnp.where(
        lane_ids(8, channels) // HEAD == row_ids(8, channels), 1.0, 0.0
    ).astype(jnp.float32)

    def load(a, carry):
        rows = pl.ds(pl.multiple_of(a * size, size), size)
        padded = pl.ds(pl.multiple_of(a * size + 8, 8), size)
        block = piece_at(a, at)
        xpad[padded] = proj_ref[block, :, :channels]
        bpad[padded] = proj_ref[block, :, tail : tail + states]
        d_scan = dcomb_ref[rows].astype(half_type)
        dsc[rows] = d_scan
        d_full = d_scan.astype(jnp.float32)
        dst[:, rows] = d_full.T.astype(half_type)
        cbt[:, rows] = basis_ref[rows, state:].astype(jnp.float32).T.astype(half_type)
        xpre = xpre_ref[rows]
        mixed = (xpre * jax.nn.sigmoid(xpre)).astype(half_type).astype(jnp.float32)
        mixt[:, rows] = mixed.T
        qrow[:, rows] = dot_nt(head_of, d_full * scan_ref[rows], precision=lax.Precision.HIGHEST)
        return carry

    lax.fori_loop(0, blocks, load, 0)

    def row_block(i, carry):
        rows_t = pl.ds(pl.multiple_of(i * size, size), size)
        basis_c = basis_ref[rows_t, state:]
        seg_t = segc_ref[rows_t]
        columns = cols_ref[rows_t]

        def pair_block(j, total):
            rows_s = pl.ds(pl.multiple_of(j * size, size), size)
            allowed = pair_mask(seg_t, segr_ref[:, rows_s], i, j)
            gram = jnp.where(allowed, dot_nt(basis_c, basis_ref[rows_s, :state]), 0.0)
            cum_s = rows_ref[8:16, rows_s]
            d_gram = jnp.zeros((size, size), jnp.float32)
            for pair in range(heads // 2):
                span = slice(pair * 128, pair * 128 + 128)
                values = inputs_ref[rows_s, span]
                d_scan = dsc[rows_t, span]
                for h in (2 * pair, 2 * pair + 1):
                    mine = (lanes < HEAD) if h % 2 == 0 else (lanes >= HEAD)
                    spread = columns[:, 8 + h : 9 + h] - cum_s[h : h + 1]
                    decay = jnp.exp(jnp.minimum(spread, 0.0))
                    weights = (gram * decay).astype(half_type)
                    d_weights = dot_nt(jnp.where(mine, d_scan, jnp.zeros_like(d_scan)), values)
                    d_gram = d_gram + d_weights * decay
                    chans = slice(h * HEAD, h * HEAD + HEAD)
                    dint[chans, rows_s] += dot_nn(dst[chans, rows_t], weights)
            d_gram = jnp.where(allowed, d_gram, 0.0).astype(half_type)
            dbt[:, rows_s] += dot_nn(cbt[:, rows_t], d_gram)
            return total + dot_nn(d_gram, basis_ref[rows_s, :state])

        dcb[rows_t] = lax.fori_loop(0, i + 1, pair_block, jnp.zeros((size, state), jnp.float32))
        return carry

    lax.fori_loop(0, blocks, row_block, 0)

    step_size = rows_ref[0:8]
    raw = rows_ref[16:24]
    d_step, col_part = [], []
    for h in range(heads):
        chans = slice(h * HEAD, h * HEAD + HEAD)
        d_inputs = dint[chans]
        mixed = mixt[chans]
        scaled = step_size[h : h + 1] * mixed
        d_step.append(jnp.sum(d_inputs * mixed, axis=0, keepdims=True))
        inputs = scaled.astype(half_type).astype(jnp.float32)
        col_part.append(jnp.sum(d_inputs * inputs, axis=0, keepdims=True))
        dint[chans] = d_inputs * step_size[h : h + 1]
    blank = jnp.zeros((8 - heads, length), jnp.float32)
    d_step = jnp.concatenate(d_step + [blank], axis=0)
    d_cum = qrow[...] - jnp.concatenate(col_part + [blank], axis=0)
    d_log = scan_lanes(d_cum, True)
    rate = jnp.exp(rate_ref[:, 1:2])
    grad_rate = jnp.sum(d_log * (-step_size * rate), axis=1, keepdims=True)
    d_raw = (d_step - d_log * rate) * jax.nn.sigmoid(raw)
    d_raw = jnp.where(row_ids(8, length) < heads, d_raw, 0.0)
    grad_bias = jnp.sum(d_raw, axis=1, keepdims=True)
    lanes8 = lane_ids(8, 128)
    grads_ref[...] = jnp.where(lanes8 == 0, grad_bias, jnp.where(lanes8 == 1, grad_rate, 0.0))
    qrow[...] = d_raw

    def grad_block(a, carry):
        rows = pl.ds(pl.multiple_of(a * size, size), size)
        d_mixed = dint[:, rows].T + dcomb_ref[rows] * gain_ref[1:2]
        dpx[rows] = d_mixed * silu_slope(xpre_ref[rows])
        d_basis = jnp.concatenate([dbt[:, rows].T, dcb[rows]], axis=1)
        dpb[rows] = d_basis * silu_slope(bpre_ref[rows])
        return carry

    lax.fori_loop(0, blocks, grad_block, 0)

    def conv_block(a, carry):
        grad_x, grad_b = carry
        rows = pl.ds(pl.multiple_of(a * size, size), size)
        window = pl.ds(pl.multiple_of(a * size, size), size + 8)
        block = piece_at(a, at)
        keep_window = keep_ref[window]
        keep = keep_window[:size]
        d_wide = dpx[window]
        dproj_ref[block, :, :channels] = conv_back(d_wide, keep_window, taps_ref[...]).astype(
            half_type
        )
        grad_x = grad_x + conv_grads(d_wide[:size], xpad[window], keep)
        d_wide = dpb[window]
        dproj_ref[block, :, channels : channels + states] = conv_back(
            d_wide, keep_window, tapb_ref[...]
        ).astype(half_type)
        grad_b = grad_b + conv_grads(d_wide[:size], bpad[window], keep)
        d_steps = jnp.concatenate([qrow[:, rows], jnp.zeros((120, size), jnp.float32)], axis=0)
        dproj_ref[block, :, channels + states :] = d_steps.T.astype(half_type)
        return grad_x, grad_b

    grad_x, grad_b = lax.fori_loop(
        0,
        blocks,
        conv_block,
        (jnp.zeros((8, channels), jnp.float32), jnp.zeros((8, states), jnp.float32)),
    )
    gradx_ref[...] = grad_x
    gradb_ref[...] = grad_b


def stack_rows(pieces, out_ref):
    begin_at = 0
    for piece in pieces:
        out_ref[begin_at : begin_at + piece.shape[0]] = piece[...]
        begin_at = begin_at + piece.shape[0]


def project_body(count, order_ref, *refs):
    pieces, parts = refs[:4], refs[4 : 4 + count]
    first_ref, proj_ref, weight_ref, small_ref, taps_ref = refs[4 + count :]
    width = weight_ref.shape[0]
    rows = proj_ref.shape[1]
    states = taps_ref.shape[1]
    stack_rows(parts, weight_ref)
    small = weight_ref[:, weight_ref.shape[1] - 128 :].astype(jnp.float32).T[8:16]
    small_ref[...] = small
    gain = small[0:1]
    for p, piece in enumerate(pieces):
        first = (piece[:rows].astype(jnp.float32) * gain).astype(jnp.bfloat16)
        first_ref[p] = first
        proj_ref[p] = dot_nn(first, weight_ref[...])
    feature = row_ids(width, states)
    block = width // 8
    place = feature % block
    for b in range(8):
        place = place + jnp.where(feature // block == b, order_ref[b] * block, 0)
    channel = lane_ids(width, states)
    taps = []
    for k in range(CONV + 1):
        picked = jnp.where(place == channel * CONV + k % CONV, 1.0, 0.0).astype(jnp.bfloat16)
        found = dot_nn(small.astype(jnp.bfloat16), picked)
        taps.append(found[2:3] if k < CONV else found[3:4])
    taps.append(jnp.zeros((8 - len(taps), states), jnp.float32))
    taps_ref[...] = jnp.concatenate(taps, axis=0)


def product_body(_, values_ref, weight_ref, keep_ref, give_ref):
    rows = values_ref.shape[1]
    columns = slice(weight_ref.shape[1] - values_ref.shape[2], None)
    for p in (3, 1, 2, 0):
        result = dot_nt(values_ref[p], weight_ref[:, columns])
        if p < 2:
            keep_ref[p * rows : p * rows + rows] = result
        else:
            give_ref[p * rows - 2 * rows : p * rows - rows] = result.astype(jnp.bfloat16)


def first_back_body(_, attn_ref, scan_ref, late_ref, weight_ref, keep_ref, give_ref):
    rows = attn_ref.shape[1]
    wide = attn_ref.shape[2] - 128
    channels = wide - 128
    for p in (3, 1, 2, 0):
        result = dot_nt(attn_ref[p, :, :wide], late_ref[:, :wide])
        result = result + dot_nt(attn_ref[p, :, wide:], weight_ref[:, channels:wide])
        result = result + dot_nt(scan_ref[p, :, :channels], weight_ref[:, :channels])
        result = result + dot_nt(scan_ref[p, :, channels:], weight_ref[:, wide:])
        if p < 2:
            keep_ref[p * rows : p * rows + rows] = result
        else:
            give_ref[p * rows - 2 * rows : p * rows - rows] = result.astype(jnp.bfloat16)


def ffn_body(slots, fresh, _, *refs):
    pieces, cots = refs[0:2], refs[2:4]
    if fresh:
        parts, outs = refs[4:-7], refs[-7:]
        weight_ref = outs[6]
        stack_rows(parts, weight_ref)
    else:
        weight_ref, outs = refs[4], refs[-6:]
    second_ref, cot_ref, hidden_ref, dgu_ref, dkeep, dgive = outs[:6]
    hidden_local = hidden_ref.shape[2]
    rows = second_ref.shape[1]
    gate_up_weight = weight_ref.at[:, : 2 * hidden_local]
    down_weight = weight_ref.at[:, 2 * hidden_local :]
    for p, piece, cots_ref in zip(slots, pieces, cots):
        values, cot = piece[...], cots_ref[rows:]
        second_ref[p] = values
        cot_ref[p] = cot
        gate_up = dot_nn(values, gate_up_weight[...])
        d_hidden = dot_nn(cot, down_weight[...])
        gate, up = gate_up[:, :hidden_local], gate_up[:, hidden_local:]
        sig = jax.nn.sigmoid(gate)
        act = gate * sig
        hidden = (act * up).astype(jnp.bfloat16)
        hidden_ref[p] = hidden
        d_gate = (d_hidden * up * sig * (1.0 + gate * (1.0 - sig))).astype(jnp.bfloat16)
        d_up = (d_hidden * act).astype(jnp.bfloat16)
        dgu_ref[p, :, :hidden_local] = d_gate
        dgu_ref[p, :, hidden_local:] = d_up
        d_second = dot_nt(dgu_ref[p], gate_up_weight[...])
        if p < 2:
            dkeep[...] = d_second
        else:
            dgive[...] = d_second.astype(jnp.bfloat16)


def pack_body(turned, _, *refs):
    out_ref = refs[-1]
    begin_at = 0
    for index, ref in enumerate(refs[:-1]):
        values = ref[...]
        if index in turned:
            values = values.T
        out_ref[:, begin_at : begin_at + values.shape[1]] = values.astype(jnp.bfloat16)
        begin_at = begin_at + values.shape[1]


def shared_body(at_ref, mine_ref, near_ref, far_ref, cross_ref, step_ref, out_ref):
    at = at_ref[0]
    rows = mine_ref.shape[0]
    lanes = lane_ids(rows, 128)
    states = mine_ref.shape[1] - 384
    for j, ref in enumerate((mine_ref, near_ref, far_ref, cross_ref)):
        values = ref[...].astype(jnp.float32)
        here = pl.ds(pl.multiple_of((at ^ j) * rows, rows), rows)
        key, value = values[:, :128], values[:, 128:256]
        low = jnp.where(lanes < HEAD, key, pltpu.roll(value, HEAD, 1))
        high = jnp.where(lanes < HEAD, pltpu.roll(key, HEAD, 1), value)
        out_ref[here, :128] = jnp.where(at < 2, low, high).astype(jnp.bfloat16)
        out_ref[here, 128 : 128 + states] = values[:, 256 : 256 + states].astype(jnp.bfloat16)
        out_ref[here, 128 + states :] = (
            values[:, 256 + states :] + step_ref[here]
        ).astype(jnp.bfloat16)


def call_kernel(body, outs, scratch, *args, deps=(), micros=2, limit=32, aliases=None):
    shapes = [jax.ShapeDtypeStruct(shape, kind) for shape, kind in outs]
    count, extra = len(args), len(deps)
    whole = pl.BlockSpec(memory_space=pltpu.VMEM)

    def wrapped(*refs):
        body(*refs[:count], *refs[count + extra :])

    return pl.pallas_call(
        wrapped,
        out_shape=shapes,
        in_specs=[pl.BlockSpec(memory_space=pltpu.SMEM)]
        + [whole] * (count - 1)
        + [pl.BlockSpec(memory_space=pl.ANY)] * extra,
        out_specs=[whole] * len(shapes),
        scratch_shapes=[pltpu.VMEM(shape, kind) for shape, kind in scratch],
        input_output_aliases=aliases or {},
        compiler_params=pltpu.CompilerParams(vmem_limit_bytes=limit * 2**20),
        cost_estimate=pl.CostEstimate(
            flops=int(micros * 1e9), bytes_accessed=0, transcendentals=0
        ),
    )(*args, *deps)


def sequence_tables(seg_ids):
    length = seg_ids.shape[0]
    places = jnp.arange(length, dtype=jnp.int32)
    starts = jnp.where((places == 0) | (seg_ids != jnp.roll(seg_ids, 1)), places, 0)
    position = places - lax.cummax(starts, axis=0)
    half_dim = HEAD // 2
    frequency = jnp.exp(-jnp.log(ROPE_BASE) * jnp.arange(half_dim, dtype=jnp.float32) / half_dim)
    angles = position.astype(jnp.float32)[:, None] * frequency[None, :]
    cosine, sine = jnp.cos(angles), jnp.sin(angles)
    cosine = jnp.concatenate([cosine] * 4, axis=1)
    sine = jnp.concatenate([-sine, sine] * 2, axis=1)
    masks = [jnp.ones((length,), jnp.float32)]
    for lag in range(1, CONV):
        masks.append(
            ((places >= lag) & (seg_ids == jnp.roll(seg_ids, lag))).astype(jnp.float32)
        )
    masks = jnp.stack(masks + [jnp.zeros((length,), jnp.float32)] * (8 - CONV), axis=1)
    return cosine, sine, jnp.pad(masks, ((0, 8), (0, 0)))


def tap_rows(kernel, offset):
    taps = jnp.concatenate([kernel.T, offset[None, :]], axis=0)
    return jnp.pad(taps, ((0, 8 - taps.shape[0]), (0, 0)))


def shards(
    tokens,
    segment_ids,
    cotangent,
    norm_gain,
    w_z,
    w_x,
    w_bc,
    w_dt,
    conv_x,
    conv_bias_x,
    conv_bc,
    conv_bias_bc,
    dt_bias,
    a_log,
    d_skip,
    mixer_gain,
    w_mixer_out,
    w_query,
    w_keyval,
    w_attn_out,
    ffn_gain,
    w_gate,
    w_up,
    w_down,
):
    half_type = jnp.bfloat16
    full_type = jnp.float32
    rows, width = tokens.shape
    length = segment_ids.shape[0]
    channels = w_z.shape[1]
    heads = w_dt.shape[1]
    hidden_local = w_gate.shape[1]
    states = 2 * STATE
    blocks = length // rows

    row_count = w_bc.shape[0]
    gain_rows = norm_gain.shape[0]
    conv_rows = conv_bc.shape[0]
    at = lax.axis_index("tp").astype(jnp.int32).reshape(1)
    order = feature_order()
    x_at, core_at = place_bits()
    x_core = jnp.zeros((1,), jnp.int32)

    small = jnp.stack([norm_gain, ffn_gain, conv_bc.reshape(-1), jnp.repeat(conv_bias_bc, CONV)], 1)
    shared_in = jnp.concatenate(
        [w_keyval, w_bc, jnp.pad(small, ((0, 0), (8, 116)))], axis=1
    ).astype(half_type)
    step_wide = jnp.pad(w_dt, ((0, 0), (0, 128 - heads)))
    if staged():
        mine, far, near, cross = gather_pieces(shared_in)
        (shared_shard,) = call_kernel(
            shared_body,
            [((4 * row_count, states + 256), half_type)],
            [],
            at,
            mine,
            near,
            far,
            cross,
            step_wide,
            micros=1,
        )
    else:
        shared_all = lax.all_gather(shared_in, "tp", axis=0, tiled=True)
        key_rows, value_rows = (
            jnp.where(x_at == 0, shared_all[:, k : k + HEAD], shared_all[:, k + HEAD : k + 2 * HEAD])
            for k in (0, 128)
        )
        shared_shard = jnp.concatenate(
            [
                key_rows,
                value_rows,
                shared_all[:, 256 : 256 + states],
                shared_all[:, 256 + states :] + step_wide.astype(half_type),
            ],
            axis=1,
        )
    def pack(turned, *shards, deps=()):
        width_all = sum(shard.size for shard in shards) // w_x.shape[0]
        return call_kernel(
            functools.partial(pack_body, turned),
            [((w_x.shape[0], width_all), half_type)],
            [],
            x_core,
            *shards,
            deps=deps,
            micros=1,
        )[0]

    gather = Gather(jnp.concatenate([w_x.astype(half_type), shared_shard], axis=1))
    both_mine, tok_rows = call_kernel(
        front_body,
        [((2 * rows, width), half_type), ((rows, width), half_type)],
        [],
        order,
        tokens,
        cotangent,
        deps=[far] if staged() else [],
    )
    both = gather_pieces(both_mine)
    gather.step()
    second_step = gather.step()
    gather.step()
    late_gather = Gather(pack((2, 3), w_z, w_query, w_mixer_out, w_attn_out, deps=second_step))
    first_step = late_gather.step()
    second_step = late_gather.step()
    late_gather.step()
    ffn_gather = Gather(pack((2,), w_gate, w_up, w_down, deps=second_step))
    ffn_first = ffn_gather.step()

    cosine, sine, keep_masks = sequence_tables(segment_ids)
    seg_col, seg_row = segment_ids[:, None], segment_ids[None, :]
    taps_x = tap_rows(conv_x, conv_bias_x)
    rates = jnp.pad(jnp.stack([dt_bias, a_log], axis=1), ((0, 8 - heads), (0, 126)))
    gains = jnp.stack([mixer_gain, jnp.repeat(d_skip, channels // heads)])
    gains = jnp.pad(gains, ((0, 6), (0, 0)))

    row_half = ((rows, width), half_type)
    row_full = ((rows, width), full_type)
    parts = gather.parts()
    columns = channels + 128 + states + 128
    first_in, proj, weight, small_rows, taps_bc = call_kernel(
        functools.partial(project_body, len(parts)),
        [
            ((blocks, rows, width), half_type),
            ((blocks, rows, columns), full_type),
            ((width, columns), half_type),
            ((8, width), full_type),
            ((8, states), full_type),
        ],
        [],
        order,
        *both,
        *parts,
        micros=6,
    )
    gain_one, gain_two = small_rows[0:1], small_rows[1:2]

    scan_out, x_pre, bc_pre, basis, inputs, time_rows, time_cols = call_kernel(
        functools.partial(ssd_forward_body, heads),
        [
            ((length, channels), full_type),
            ((length, channels), full_type),
            ((length, states), full_type),
            ((length, states), half_type),
            ((length, channels), half_type),
            ((24, length), full_type),
            ((length, 128), full_type),
        ],
        [
            ((length + 8, channels), full_type),
            ((length + 8, states), full_type),
            ((8, length), full_type),
        ],
        at,
        proj,
        seg_col,
        seg_row,
        keep_masks,
        taps_x,
        taps_bc,
        rates,
        deps=[*first_step, *second_step],
        micros=11,
    )
    parts = late_gather.parts()
    head_half = ((length, 128), half_type)
    head_full = ((length, 128), full_type)
    cat, gate_in, query, keyk, valv, logs, inverse, late_weight = call_kernel(
        functools.partial(attend_forward_body, len(parts)),
        [
            ((blocks, rows, channels + 128), half_type),
            ((blocks, rows, channels), full_type),
            head_half,
            head_half,
            head_half,
            head_full,
            head_full,
            ((width, 2 * (channels + 128)), half_type),
        ],
        [],
        at,
        first_in,
        proj,
        scan_out,
        x_pre,
        seg_col,
        seg_row,
        cosine,
        sine,
        gains,
        *parts,
        deps=ffn_first,
        micros=9,
    )
    ffn_second = ffn_gather.step()

    def row_products(values, weight, deps=()):
        return call_kernel(
            product_body,
            [((2 * rows, width), full_type), ((2 * rows, width), half_type)],
            [],
            x_core,
            values,
            weight,
            deps=deps,
        )

    mix_terms = reduce_pieces(*row_products(cat, late_weight, deps=ffn_second))
    ffn_third = ffn_gather.step()
    after_mix, second_mine = call_kernel(
        mixed_body,
        [row_full, row_half],
        [],
        order,
        tok_rows,
        *mix_terms,
        gain_two,
        deps=ffn_third,
    )
    second = gather_pieces(second_mine)

    parts = ffn_gather.parts()
    filled = [
        ((blocks, rows, width), half_type),
        ((blocks, rows, width), half_type),
        ((blocks, rows, hidden_local), half_type),
        ((blocks, rows, 2 * hidden_local), half_type),
    ]
    sums = [row_full, row_half]
    *filled_in, d_keep, d_give, ffn_weight = call_kernel(
        functools.partial(ffn_body, (0, 2), True),
        filled + sums + [((width, 3 * hidden_local), half_type)],
        [],
        x_core,
        second[0],
        second[2],
        both[0],
        both[2],
        *parts,
        micros=5,
    )
    *filled_in, d_keep_x, d_give_x = call_kernel(
        functools.partial(ffn_body, (1, 3), False),
        filled + sums,
        [],
        x_core,
        second[1],
        second[3],
        both[1],
        both[3],
        ffn_weight,
        *filled_in,
        micros=5,
        aliases={6: 0, 7: 1, 8: 2, 9: 3},
    )
    second_in, cot_all, hidden, d_gate_up = (
        array.reshape(length, array.shape[2]) for array in filled_in
    )
    near = flip(d_give, "tp", 1)
    passed = d_keep_x + flip(d_give_x, "tp", 1).astype(full_type)
    d_second = d_keep, near, flip(passed.astype(half_type), "tp", 2)
    ffn_scatter = Scatter(
        [
            contract_rows(second_in, d_gate_up).astype(half_type),
            contract_rows(cot_all, hidden).astype(half_type),
        ]
    )

    d_after, d_mix = call_kernel(
        after_back_body,
        [row_full, row_half],
        [],
        order,
        after_mix,
        both_mine,
        *d_second,
        gain_two,
    )
    d_mix_all = gather_pieces(d_mix)
    ffn_steps = [ffn_scatter.step(3)]

    d_attn, d_comb, sums_mix, d_mix_whole = call_kernel(
        attend_backward_body,
        [
            ((blocks, rows, channels + 256), half_type),
            ((length, channels), full_type),
            ((8, channels), full_type),
            ((blocks, rows, width), half_type),
        ],
        [
            ((length, 128), full_type),
            ((length, 128), full_type),
            ((blocks, rows, channels + 128), full_type),
        ],
        at,
        gate_in,
        *d_mix_all,
        late_weight,
        scan_out,
        x_pre,
        seg_col,
        seg_row,
        cosine,
        sine,
        gains,
        query,
        keyk,
        valv,
        logs,
        inverse,
        deps=ffn_steps[0],
        micros=10,
    )
    ffn_steps.append(ffn_scatter.step(2))
    out_terms = reduce_pieces(*row_products(filled_in[2], ffn_weight, deps=d_mix_all[1:]))
    first_rows = first_in.reshape(length, width)
    attn_scatter = Scatter(
        [
            contract_rows(first_rows, d_attn.reshape(length, channels + 256)).astype(half_type),
            contract_rows(
                d_mix_whole.reshape(length, width), cat.reshape(length, channels + 128)
            ).astype(half_type),
        ]
    )
    d_scan, sums_x, sums_bc, sums_rate = call_kernel(
        functools.partial(ssd_backward_body, heads),
        [
            ((blocks, rows, channels + states + 128), half_type),
            ((8, channels), full_type),
            ((8, states), full_type),
            ((8, 128), full_type),
        ],
        [
            ((length + 8, channels), full_type),
            ((length + 8, states), full_type),
            ((length + 8, channels), full_type),
            ((length + 8, states), full_type),
            ((length, channels), half_type),
            ((channels, length), half_type),
            ((STATE, length), half_type),
            ((channels, length), full_type),
            ((channels, length), full_type),
            ((STATE, length), full_type),
            ((length, STATE), full_type),
            ((8, length), full_type),
        ],
        at,
        proj,
        d_comb,
        scan_out,
        seg_col,
        seg_row,
        keep_masks,
        taps_x,
        taps_bc,
        rates,
        gains,
        x_pre,
        bc_pre,
        basis,
        inputs,
        time_rows,
        time_cols,
        deps=ffn_steps[1],
        micros=18,
    )
    ffn_steps.append(ffn_scatter.step(1))
    ffn_sum = ffn_scatter.total()
    scan_scatter = Scatter(
        [
            contract_rows(
                first_rows, d_scan.reshape(length, channels + states + 128)
            ).astype(half_type)
        ]
    )
    keep, give = call_kernel(
        first_back_body,
        [((2 * rows, width), full_type), ((2 * rows, width), half_type)],
        [],
        x_core,
        d_attn,
        d_scan,
        late_weight,
        weight,
        deps=[out_terms[2]],
        micros=4,
    )
    d_first = reduce_pieces(keep, give)
    (grad_tokens,) = call_kernel(
        token_back_body,
        [row_full],
        [],
        order,
        tok_rows,
        d_after,
        *d_first,
        gain_one,
    )

    for dz in (3, 2, 1):
        attn_scatter.step(dz)
        scan_scatter.step(dz)
    attn_sum = attn_scatter.total()
    scan_sum = scan_scatter.total()
    out_sum = attn_sum[:, channels + 256 :]
    attn_sum = attn_sum[:, : channels + 256]

    (layer_out,) = call_kernel(
        output_body,
        [row_half],
        [],
        order,
        after_mix,
        *out_terms,
    )
    sum_x, sum_bc, sum_step = split_cols(scan_sum, [channels, states, heads])
    bc_rows = shared_shard[:, 128 : 128 + states]
    sum_z, sum_query, sum_keyval = split_cols(attn_sum, [channels, 128, 128])
    shared_rows = jnp.concatenate([sum_bc, sum_keyval], axis=1)
    shared_rows = shared_rows.reshape(2, 2, row_count, shared_rows.shape[1])
    keep = jnp.where(core_at == 0, shared_rows[:, 0], shared_rows[:, 1])
    give = jnp.where(core_at == 0, shared_rows[:, 1], shared_rows[:, 0])
    chip_rows = keep + flip(give, "tp", 1)
    keep = jnp.where(x_at == 0, chip_rows[0], chip_rows[1])
    give = jnp.where(x_at == 0, chip_rows[1], chip_rows[0])
    came = flip(give, "tp", 2)
    grad_bc = keep[:, :states] + came[:, :states]
    key_mine, value_mine = split_cols(keep[:, states:], [HEAD, HEAD])
    key_came, value_came = split_cols(came[:, states:], [HEAD, HEAD])
    grad_keyval = jnp.where(
        x_at == 0,
        jnp.concatenate([key_mine, key_came, value_mine, value_came], axis=1),
        jnp.concatenate([key_came, key_mine, value_came, value_mine], axis=1),
    )

    def weighted(grads, weights):
        weights = jnp.concatenate([weight.astype(half_type) for weight in weights], axis=1)
        return jnp.sum(grads * weights.astype(full_type), axis=1)

    by_row = [
        weighted(scan_sum[:, : channels + states + heads], [w_x, bc_rows[:, :states], w_dt])
        + weighted(attn_sum, [w_z, w_query, shared_shard[:, :128]]),
        weighted(ffn_sum[:, : 2 * hidden_local], [w_gate, w_up]),
    ]
    by_row = sum_tp(jnp.stack(by_row)).reshape(2, 4, gain_rows)
    by_row = lax.dynamic_index_in_dim(by_row, lax.axis_index("tp"), 1, keepdims=False)
    rounded = [gain.astype(half_type).astype(full_type) for gain in (norm_gain, ffn_gain)]
    sum_gain_one, sum_gain_two = by_row[0] / rounded[0], by_row[1] / rounded[1]

    common = sums_bc.reshape(-1)
    skips = sums_mix[1].reshape(heads, channels // heads).sum(axis=1)
    parts = [sums_x[:5].reshape(-1), sums_rate[:, :2].reshape(-1), skips, sums_mix[0]]
    flat = jnp.concatenate([sum_tp(common)] + parts)
    flat = jnp.pad(flat, (0, -flat.shape[0] % 1024)).reshape(-1, 128)
    flat = sum_fsdp(flat).reshape(-1)
    bc_sums = flat[: common.shape[0]].reshape(8, states)
    flat = flat[common.shape[0] :]
    device = lax.axis_index("fsdp") * 4 + lax.axis_index("tp")
    sum_conv = lax.dynamic_slice_in_dim(bc_sums[:4].T, device * conv_rows, conv_rows)
    sum_bias = lax.dynamic_slice_in_dim(bc_sums[4], device * conv_rows, conv_rows)
    x_sums = flat[: 5 * channels].reshape(5, channels)
    flat = flat[5 * channels :]
    rate_sums = flat[:16].reshape(8, 2)[:heads]
    skip_sums = flat[16 : 16 + heads]
    gain_sums = flat[16 + heads : 16 + heads + channels]
    sum_gate, sum_up, sum_down = split_cols(ffn_sum, [hidden_local] * 3)
    return (
        layer_out,
        grad_tokens,
        sum_gain_one,
        sum_z,
        sum_x,
        grad_bc,
        sum_step,
        x_sums[:4].T,
        x_sums[4],
        sum_conv,
        sum_bias,
        rate_sums[:, 0],
        rate_sums[:, 1],
        skip_sums,
        gain_sums,
        out_sum[:, :channels].T,
        sum_query,
        grad_keyval,
        out_sum[:, channels:].T,
        sum_gain_two,
        sum_gate,
        sum_up,
        sum_down.T,
    )


def solution(mesh):
    placed = (
        P(("fsdp", "tp"), None),
        P("fsdp"),
        P(("fsdp", "tp"), None),
        P(("fsdp", "tp")),
        P("fsdp", "tp"),
        P("fsdp", "tp"),
        P(("fsdp", "tp"), None),
        P("fsdp", "tp"),
        P("tp", None),
        P("tp"),
        P(("fsdp", "tp"), None),
        P(("fsdp", "tp")),
        P("tp"),
        P("tp"),
        P("tp"),
        P("tp"),
        P("tp", "fsdp"),
        P("fsdp", "tp"),
        P(("fsdp", "tp"), None),
        P("tp", "fsdp"),
        P(("fsdp", "tp")),
        P("fsdp", "tp"),
        P("fsdp", "tp"),
        P("tp", "fsdp"),
    )
    return jax.shard_map(
        shards,
        mesh=mesh,
        in_specs=placed,
        out_specs=(
            P(("fsdp", "tp"), None),
            P(("fsdp", "tp"), None),
            P(("fsdp", "tp")),
            P("fsdp", "tp"),
            P("fsdp", "tp"),
            P(("fsdp", "tp"), None),
            P("fsdp", "tp"),
            P("tp", None),
            P("tp"),
            P(("fsdp", "tp"), None),
            P(("fsdp", "tp")),
            P("tp"),
            P("tp"),
            P("tp"),
            P("tp"),
            P("tp", "fsdp"),
            P("fsdp", "tp"),
            P(("fsdp", "tp"), None),
            P("tp", "fsdp"),
            P(("fsdp", "tp")),
            P("fsdp", "tp"),
            P("fsdp", "tp"),
            P("tp", "fsdp"),
        ),
        check_vma=False,
    )
```

time: 639 us -> 399 us (0.62)
  other arithmetic: 134 us -> 41.9 us
  matrix products: 97.3 us -> 8.72 us
  Pallas kernels: 0 us -> 86.6 us
  local copies, waits for them, and re-layouts: 134 us -> 53.7 us
  starting transfers between devices: 80.7 us -> 49.3 us
  waiting for transfers between devices: 179 us -> 151 us
    pallas_call x0 -> x18, Pallas kernels: none -> 86.6 us  [call_kernel(): pl.pallas_call(wrapped, out_shape=shapes, in_specs=[pl.BlockSpec(memory_s...]
    dot_general x19 -> x0, matrix products: 85.1 us -> none  [the longest x1 17.3 us: mix_backward(): jnp.einsum('thp,shp->hts', d_scan_half, inputs_mat, preferred_element_typ...]
    ppermute x34 -> x18, waiting for transfers between devices: 129 us -> 69.5 us  [ring(): lax.ppermute(values, 'fsdp', [(i, (i + 2 * step) % 8) for i in range(8)])]
    ppermute x34 -> x18, starting transfers between devices: 54.4 us -> 4.84 us  [ring(): lax.ppermute(values, 'fsdp', [(i, (i + 2 * step) % 8) for i in range(8)])]
    ppermute x37 -> x54, waiting for transfers between devices: 49.7 us -> 81.9 us  [flip(): return lax.ppermute(values, axis, [(i, i ^ mask) for i in range(size)])]
    reshape x20 -> x3, local copies, waits for them, and re-layouts: 29.4 us -> 0.16 us  [the longest x1 0.08 us: shards(): by_row = sum_tp(jnp.stack(by_row)).reshape(2, 4, gain_rows)]
    reduce_sum x9 -> x4, other arithmetic: 25 us -> 2.15 us  [the longest x3 2.03 us: weighted(): return jnp.sum(grads * weights.astype(full_type), axis=1)]
    select_n x30 -> x0, other arithmetic: 22 us -> none  [the longest x6 7.87 us: causal_conv(): jnp.where(conv_keep[lag_step - 1], shifted, 0.0)]
  transfers between devices with their start and end apart: 71 -> 72, of which waited for: 31 -> 38; matrix products, arithmetic and copies ran while one was open for 42% -> 17% of each run, Pallas kernels for 0% -> 18%
where the time goes in v2:
time: 399 us; the launch traced here: 394 us
  waiting for transfers between devices  151 us (38%)
  Pallas kernels  86.6 us (22%)
  local copies, waits for them, and re-layouts  53.7 us (13%)
  starting transfers between devices  49.3 us (12%)
  other arithmetic  41.9 us (11%)
  matrix products  8.72 us (2%)
    pallas_call x18, Pallas kernels, call_kernel(): pl.pallas_call(wrapped, out_shape=shapes, in_specs=[pl.BlockSpec(memory_s...  86.6 us
    ppermute x54, waiting for transfers between devices, flip(): return lax.ppermute(values, axis, [(i, i ^ mask) for i in range(size)])  81.9 us
    ppermute x18, waiting for transfers between devices, ring(): lax.ppermute(values, 'fsdp', [(i, (i + 2 * step) % 8) for i in range(8)])  69.5 us
    ppermute x54, starting transfers between devices, flip(): return lax.ppermute(values, axis, [(i, i ^ mask) for i in range(size)])  44.4 us
    unnamed x250, local copies, waits for them, and re-layouts  34.4 us
    convert_element_type x9, other arithmetic, step(): self.carried = ring(self.summed(dz).astype(jnp.bfloat16), 1)  9.27 us
    dot_general x5, matrix products, contract_rows(): lax.dot_general(left_side, right_side, (((0,), (0,)), ((), ())), preferre...  8.72 us
  transfers between devices with their start and end apart: 72, of which 38 were waited for; matrix products, arithmetic and copies ran while one was open for 17% of the time, Pallas kernels for 18%

profile of v2, /device:TPU:0, one launch (start us, length us, event | category | flops | bytes accessed | tf_op | source)
XLA Modules:
  0.0 393.9 jit_solution(1577271910531852053)
XLA Ops:
  14.2 8.2 %collective-permute-done.6.refs_8_ = bf16[128,896]{1,0:T(8,128)(2,1)S(1)} collective-permute-done((bf16[128,896]{1,0:T(8,128)(2,1)S(1)}, bf16[128,896]{1,0:T(8,128)(2,1)S(1)}, u32[]{:S(2)}, u32[]{:S(2)}) %collective-permute-start.6) | collective-permute-done | bytes 229408 | tf_op jit(solution)/shard_map/ppermute | solution.py:48
  27.4 4.3 %collective-permute-done.7.refs_7_.refs_5_ = bf16[128,896]{1,0:T(8,128)(2,1)S(1)} collective-permute-done((bf16[128,896]{1,0:T(8,128)(2,1)S(1)}, bf16[128,896]{1,0:T(8,128)(2,1)S(1)}, u32[]{:S(2)}, u32[]{:S(2)}) %collective-permute-start.7) | collective-permute-done | bytes 229408 | tf_op jit(solution)/shard_map/ppermute | solution.py:48
  33.7 4.6 %collective-permute-done.11.refs_11_.refs_6_ = bf16[128,896]{1,0:T(8,128)(2,1)S(1)} collective-permute-done((bf16[128,896]{1,0:T(8,128)(2,1)S(1)}, bf16[128,896]{1,0:T(8,128)(2,1)S(1)}, u32[]{:S(2)}, u32[]{:S(2)}) %collective-permute-start.11) | collective-permute-done | bytes 229408 | tf_op jit(solution)/shard_map/ppermute | solution.py:44
  40.2 7.0 %collective-permute-done.13.refs_8_.refs_13_ = bf16[128,1024]{1,0:T(8,128)(2,1)S(1)} collective-permute-done((bf16[128,1024]{1,0:T(8,128)(2,1)S(1)}, bf16[128,1024]{1,0:T(8,128)(2,1)S(1)}, u32[]{:S(2)}, u32[]{:S(2)}) %collective-permute-start.13) | collective-permute-done | bytes 262176 | tf_op jit(solution)/shard_map/ppermute | solution.py:48
  51.2 4.3 %collective-permute-done.15.refs_10_.refs_4_.refs_12_ = bf16[128,1024]{1,0:T(8,128)(2,1)} collective-permute-done((bf16[128,1024]{1,0:T(8,128)(2,1)S(1)}, bf16[128,1024]{1,0:T(8,128)(2,1)}, u32[]{:S(2)}, u32[]{:S(2)}) %collective-permute-start.15) | collective-permute-done | bytes 262176 | tf_op jit(solution)/shard_map/ppermute | solution.py:48
  92.0 5.1 %shard_map.409 = (bf16[4,256,1024]{2,1,0:T(8,128)(2,1)S(1)}, f32[4,256,896]{2,1,0:T(8,128)S(1)}, bf16[1024,896]{1,0:T(8,128)(2,1)S(1)}, f32[8,1024]{1,0:T(8,128)S(1)}, f32[8,256]{1,0:T(8,128)S(1)}) custom-call(s32[8]{0:T(128)S(1)} %fusion.20.refs_0_, bf16[512,1024]{1,0:T(8,128)(2,1)} %get-tuple-element.77.refs_1_.refs_3_.refs_2_, ...), custom_call_target="tpu_custom_call" | custom-call | flops 6000000000 | tf_op jit(solution)/shard_map/pallas_call | solution.py:958
  98.4 11.0 %shard_map.411 = (f32[1024,384]{1,0:T(8,128)S(1)}, f32[1024,384]{1,0:T(8,128)S(1)}, f32[1024,256]{1,0:T(8,128)S(1)}, bf16[1024,256]{1,0:T(8,128)(2,1)S(1)}, bf16...) custom-call(s32[1]{0:T(128)} %bitcast.2.refs_0_, ...), custom_call_target="tpu_custom_call" | custom-call | flops 11000000512 | tf_op jit(solution)/shard_map/pallas_call | solution.py:958
  113.7 8.4 %shard_map.413 = (bf16[4,256,512]{2,1,0:T(8,128)(2,1)S(1)}, f32[4,256,384]{2,1,0:T(8,128)S(1)}, bf16[1024,128]{1,0:T(8,128)(2,1)S(1)}, bf16[1024,128]{1,0:T(8,12...) custom-call(s32[1]{0:T(128)} %bitcast.2.refs_0_, ...), custom_call_target="tpu_custom_call" | custom-call | flops 8999999488 | tf_op jit(solution)/shard_map/pallas_call | solution.py:958
  129.2 9.4 %collective-permute-done.26.refs_6_ = bf16[128,1536]{1,0:T(8,128)(2,1)S(1)} collective-permute-done((bf16[128,1536]{1,0:T(8,128)(2,1)S(1)}, bf16[128,1536]{1,0:T(8,128)(2,1)S(1)}, u32[]{:S(2)}, u32[]{:S(2)}) %collective-permute-start.26) | collective-permute-done | bytes 393248 | tf_op jit(solution)/shard_map/ppermute | solution.py:48
  139.4 10.1 %collective-permute-done.27.refs_7_.refs_10_ = bf16[128,1536]{1,0:T(8,128)(2,1)S(1)} collective-permute-done((bf16[128,1536]{1,0:T(8,128)(2,1)S(1)}, bf16[128,1536]{1,0:T(8,128)(2,1)S(1)}, u32[]{:S(2)}, u32[]{:S(2)}) %collective-permute-start.27) | collective-permute-done | bytes 393248 | tf_op jit(solution)/shard_map/ppermute | solution.py:44
  153.5 10.4 %collective-permute-done.28.refs_1_ = bf16[256,1024]{1,0:T(8,128)(2,1)S(1)} collective-permute-done((bf16[256,1024]{1,0:T(8,128)(2,1)S(1)}, bf16[256,1024]{1,0:T(8,128)(2,1)S(1)}, u32[]{:S(2)}, u32[]{:S(2)}) %collective-permute-start.28) | collective-permute-done | bytes 524320 | tf_op jit(solution)/shard_map/ppermute | solution.py:44
  164.2 5.0 %shard_map.416 = (bf16[4,256,1024]{2,1,0:T(8,128)(2,1)S(1)}, bf16[4,256,1024]{2,1,0:T(8,128)(2,1)S(1)}, bf16[4,256,512]{2,1,0:T(8,128)(2,1)S(1)}, bf16[4,256,102...) custom-call(s32[1]{0:T(128)} %constant.100.clone.1.refs_0_, ...), custom_call_target="tpu_custom_call" | custom-call | flops 5000000000 | tf_op jit(solution)/shard_map/pallas_call | solution.py:958
  169.2 6.1 %shard_map.417 = (bf16[4,256,1024]{2,1,0:T(8,128)(2,1)S(1)}, bf16[4,256,1024]{2,1,0:T(8,128)(2,1)S(1)}, bf16[4,256,512]{2,1,0:T(8,128)(2,1)S(1)}, bf16[4,256,102...) custom-call(s32[1]{0:T(128)} %constant.100.clone.1.refs_0_, ...), custom_call_target="tpu_custom_call", output_to_operand_aliasing={{0}: (6, {}), {1}: (7, {}), {2}: (8, {}), {3}: (9, {})} | custom-call | flops 5000000000 | tf_op jit(solution)/shard_map/pallas_call | solution.py:958
  183.4 9.3 %collective-permute-done.40 = bf16[128,1536]{1,0:T(8,128)(2,1)S(1)} collective-permute-done((bf16[128,1536]{1,0:T(8,128)(2,1)S(1)}, bf16[128,1536]{1,0:T(8,128)(2,1)S(1)}, u32[]{:S(2)}, u32[]{:S(2)}) %collective-permute-start.40) | collective-permute-done | bytes 393248 | tf_op jit(solution)/shard_map/ppermute | solution.py:44
  195.3 5.8 %collective-permute-done.42.refs_20_ = bf16[128,1536]{1,0:T(8,128)(2,1)S(1)} collective-permute-done((bf16[128,1536]{1,0:T(8,128)(2,1)S(1)}, bf16[128,1536]{1,0:T(8,128)(2,1)S(1)}, u32[]{:S(2)}, u32[]{:S(2)}) %collective-permute-start.42) | collective-permute-done | bytes 393248 | tf_op jit(solution)/shard_map/ppermute | solution.py:44
  222.5 5.0 %collective-permute-done.62 = bf16[128,1536]{1,0:T(8,128)(2,1)} collective-permute-done((bf16[128,1536]{1,0:T(8,128)(2,1)}, bf16[128,1536]{1,0:T(8,128)(2,1)}, u32[]{:S(2)}, u32[]{:S(2)}) %collective-permute-start.62) | collective-permute-done | bytes 393248 | tf_op jit(solution)/shard_map/ppermute | solution.py:48
  243.0 11.6 %shard_map.421 = (bf16[4,256,640]{2,1,0:T(8,128)(2,1)S(1)}, f32[1024,384]{1,0:T(8,128)S(1)}, f32[8,384]{1,0:T(8,128)S(1)}, bf16[4,256,1024]{2,1,0:T(8,128)(2,1)S(1)}) custom-call(s32[1]{0:T(128)} %bitcast.2.refs_0_, f32[4,256,384]{2,1,0:T(8,128)S(1)} %copy-done.72, bf16[256,1024]{1,0:T(8,128)(2,1)} %get-tuple-element.100.refs_2_, ...), custom_call_target="tpu_custom_call" | custom-call | flops 10000000000 | tf_op jit(solution)/shard_map/pallas_call | solution.py:958
  254.8 18.1 %shard_map.422 = (bf16[4,256,768]{2,1,0:T(8,128)(2,1)S(1)}, f32[8,384]{1,0:T(8,128)S(1)}, f32[8,256]{1,0:T(8,128)S(1)}, f32[8,128]{1,0:T(8,128)S(1)}) custom-call(s32[1]{0:T(128)} %bitcast.2.refs_0_, f32[4,256,896]{2,1,0:T(8,128)S(1)} %copy-done.66, f32[1024,384]{1,0:T(8,128)S(1)} %get-tuple-element.114.refs_2_, f32[1024,384]{1,0:T(8,128)S(1)} %copy-done.68, ...), custom_call_target="tpu_custom_call" | custom-call | flops 17999998976 | tf_op jit(solution)/shard_map/pallas_call | solution.py:958
  297.6 4.8 %collective-permute-done.71 = f32[40,128]{1,0:T(8,128)S(1)} collective-permute-done((f32[40,128]{1,0:T(8,128)S(1)}, f32[40,128]{1,0:T(8,128)S(1)}, u32[]{:S(2)}, u32[]{:S(2)}) %collective-permute-start.71) | collective-permute-done | bytes 20512 | tf_op jit(solution)/shard_map/ppermute | solution.py:44
  307.0 6.3 %collective-permute-done.51 = bf16[128,768]{1,0:T(8,128)(2,1)S(1)} collective-permute-done((bf16[128,768]{1,0:T(8,128)(2,1)S(1)}, bf16[128,768]{1,0:T(8,128)(2,1)S(1)}, u32[]{:S(2)}, u32[]{:S(2)}) %collective-permute-start.51) | collective-permute-done | bytes 196640 | tf_op jit(solution)/shard_map/ppermute | solution.py:48
  317.4 5.3 %collective-permute-done.52 = bf16[128,768]{1,0:T(8,128)(2,1)} collective-permute-done((bf16[128,768]{1,0:T(8,128)(2,1)}, bf16[128,768]{1,0:T(8,128)(2,1)}, u32[]{:S(2)}, u32[]{:S(2)}) %collective-permute-start.52) | collective-permute-done | bytes 196640 | tf_op jit(solution)/shard_map/ppermute | solution.py:48
  324.8 4.2 %collective-permute-done.58 = bf16[128,1152]{1,0:T(8,128)(2,1)S(1)} collective-permute-done((bf16[128,1152]{1,0:T(8,128)(2,1)}, bf16[128,1152]{1,0:T(8,128)(2,1)S(1)}, u32[]{:S(2)}, u32[]{:S(2)}) %collective-permute-start.58) | collective-permute-done | bytes 294944 | tf_op jit(solution)/shard_map/ppermute | solution.py:48
  367.4 4.0 %shard_map.423 = (f32[512,1024]{1,0:T(8,128)S(1)}, bf16[512,1024]{1,0:T(8,128)(2,1)S(1)}) custom-call(s32[1]{0:T(128)} %constant.100.clone.1.refs_0_, bf16[4,256,640]{2,1,0:T(8,128)(2,1)S(1)} %copy-done.60, bf16[4,256,768]{2,1,0:T(8,128)(2,1)S(1)} %copy-done.62, bf16[1024,1024]{1,0:T(8,128)(2,1)S(1)} %copy-done.54, bf16[1024,896]{1,0:T(8,128)(2,1)S(1)} %copy-done.64, ...), custom_call_target="tpu_custom_call" | custom-call | flops 4000000000 | tf_op jit(solution)/shard_map/pallas_call | solution.py:958
  382.2 8.4 %collective-permute-done.46.refs_5_ = bf16[256,1024]{1,0:T(8,128)(2,1)S(1)} collective-permute-done((bf16[256,1024]{1,0:T(8,128)(2,1)S(1)}, bf16[256,1024]{1,0:T(8,128)(2,1)S(1)}, u32[]{:S(2)}, u32[]{:S(2)}) %collective-permute-start.46) | collective-permute-done | bytes 524320 | tf_op jit(solution)/shard_map/ppermute | solution.py:44
  (526 shorter events, 214.9 us)
Async XLA Ops:
  25.9 25.3 %collective-permute-start.1 = (bf16[512,1024]{1,0:T(8,128)(2,1)}, bf16[512,1024]{1,0:T(8,128)(2,1)}, u32[]{:S(2)}, u32[]{:S(2)}) collective-permute-start(bf16[512,1024]{1,0:T(8,128)(2,1)} %get-tuple-element.77.refs_1_.refs_3_.refs_2_), channel_id=1, source_target_pairs={{0,2},{1,3},{2,0},{3,1},{4,6},{5,7},{6,4},{7,5},{8,10},{9,11},{10,... | collective-permute-start | bytes 3145736 | tf_op jit(solution)/shard_map/ppermute | solution.py:44
  47.4 36.0 %collective-permute-start.2 = (bf16[512,1024]{1,0:T(8,128)(2,1)}, bf16[512,1024]{1,0:T(8,128)(2,1)}, u32[]{:S(2)}, u32[]{:S(2)}) collective-permute-start(bf16[512,1024]{1,0:T(8,128)(2,1)} %get-tuple-element.77.refs_1_.refs_3_.refs_2_), channel_id=1, source_target_pairs={{0,1},{1,0},{2,3},{3,2},{4,5},{5,4},{6,7},{7,6},{8,9},{9,8},{10,11... | collective-permute-start | bytes 3145736 | tf_op jit(solution)/shard_map/ppermute | solution.py:44
  51.2 36.5 %collective-permute-start.3 = (bf16[512,1024]{1,0:T(8,128)(2,1)}, bf16[512,1024]{1,0:T(8,128)(2,1)}, u32[]{:S(2)}, u32[]{:S(2)}) collective-permute-start(bf16[512,1024]{1,0:T(8,128)(2,1)} %collective-permute-done.1.refs_2_.refs_3_), channel_id=1, source_target_pairs={{0,1},{1,0},{2,3},{3,2},{4,5},{5,4},{6,7},{7,6},{8,9},{9,8},{10,11... | collective-permute-start | bytes 3145736 | tf_op jit(solution)/shard_map/ppermute | solution.py:44
  69.0 18.3 %collective-permute-start.20 = (bf16[128,1536]{1,0:T(8,128)(2,1)S(1)}, bf16[128,1536]{1,0:T(8,128)(2,1)S(1)}, u32[]{:S(2)}, u32[]{:S(2)}) collective-permute-start(bf16[128,1536]{1,0:T(8,128)(2,1)S(1)} %shard_map.412.refs_5_), channel_id=1, source_target_pairs={{0,8},{4,12},{8,16},{12,20},{16,24},{20,28},{24,0},{28,4},{1,9},{5... | collective-permute-start | bytes 1179656 | tf_op jit(solution)/shard_map/ppermute | solution.py:48
  72.1 13.6 %collective-permute-start.17 = (bf16[128,1024]{1,0:T(8,128)(2,1)}, bf16[128,1024]{1,0:T(8,128)(2,1)}, u32[]{:S(2)}, u32[]{:S(2)}) collective-permute-start(bf16[128,1024]{1,0:T(8,128)(2,1)} %collective-permute-done.15.refs_10_.refs_4_.refs_12_), channel_id=1, source_target_pairs={{0,8},{4,12},{8,16},{12,20},{16,24},{20,28},{24,0},{28,4},{1,9},{5... | collective-permute-start | bytes 786440 | tf_op jit(solution)/shard_map/ppermute | solution.py:48
  81.9 31.8 %collective-permute-start.18 = (bf16[128,1024]{1,0:T(8,128)(2,1)}, bf16[128,1024]{1,0:T(8,128)(2,1)S(1)}, u32[]{:S(2)}, u32[]{:S(2)}) collective-permute-start(bf16[128,1024]{1,0:T(8,128)(2,1)} %copy-done.23), channel_id=1, source_target_pairs={{0,4},{4,0},{8,12},{12,8},{16,20},{20,16},{24,28},{28,24},{1,5},{5... | collective-permute-start | bytes 786440 | tf_op jit(solution)/shard_map/ppermute | solution.py:44
  83.4 15.0 %collective-permute-start.14 = (bf16[128,1024]{1,0:T(8,128)(2,1)}, bf16[128,1024]{1,0:T(8,128)(2,1)S(1)}, u32[]{:S(2)}, u32[]{:S(2)}) collective-permute-start(bf16[128,1024]{1,0:T(8,128)(2,1)} %copy-done.25), channel_id=1, source_target_pairs={{0,4},{4,0},{8,12},{12,8},{16,20},{20,16},{24,28},{28,24},{1,5},{5... | collective-permute-start | bytes 786440 | tf_op jit(solution)/shard_map/ppermute | solution.py:44
  85.7 28.0 %collective-permute-start.19 = (bf16[128,1024]{1,0:T(8,128)(2,1)}, bf16[128,1024]{1,0:T(8,128)(2,1)S(1)}, u32[]{:S(2)}, u32[]{:S(2)}) collective-permute-start(bf16[128,1024]{1,0:T(8,128)(2,1)} %collective-permute-done.17.refs_11_), channel_id=1, source_target_pairs={{0,4},{4,0},{8,12},{12,8},{16,20},{20,16},{24,28},{28,24},{1,5},{5... | collective-permute-start | bytes 786440 | tf_op jit(solution)/shard_map/ppermute | solution.py:44
  87.3 26.4 %collective-permute-start.21 = (bf16[128,1536]{1,0:T(8,128)(2,1)S(1)}, bf16[128,1536]{1,0:T(8,128)(2,1)S(1)}, u32[]{:S(2)}, u32[]{:S(2)}) collective-permute-start(bf16[128,1536]{1,0:T(8,128)(2,1)S(1)} %collective-permute-done.20.refs_18_.refs_8_), channel_id=1, source_target_pairs={{0,4},{4,0},{8,12},{12,8},{16,20},{20,16},{24,28},{28,24},{1,5},{5... | collective-permute-start | bytes 1179656 | tf_op jit(solution)/shard_map/ppermute | solution.py:44
  87.7 24.3 %collective-permute-start.22 = (bf16[128,1536]{1,0:T(8,128)(2,1)S(1)}, bf16[128,1536]{1,0:T(8,128)(2,1)S(1)}, u32[]{:S(2)}, u32[]{:S(2)}) collective-permute-start(bf16[128,1536]{1,0:T(8,128)(2,1)S(1)} %collective-permute-done.20.refs_18_.refs_8_), channel_id=1, source_target_pairs={{0,8},{4,12},{8,16},{12,20},{16,24},{20,28},{24,0},{28,4},{1,9},{5... | collective-permute-start | bytes 1179656 | tf_op jit(solution)/shard_map/ppermute | solution.py:48
  124.8 13.7 %collective-permute-start.26 = (bf16[128,1536]{1,0:T(8,128)(2,1)S(1)}, bf16[128,1536]{1,0:T(8,128)(2,1)S(1)}, u32[]{:S(2)}, u32[]{:S(2)}) collective-permute-start(bf16[128,1536]{1,0:T(8,128)(2,1)S(1)} %collective-permute-done.22.refs_3_.refs_7_), channel_id=1, source_target_pairs={{0,8},{4,12},{8,16},{12,20},{16,24},{20,28},{24,0},{28,4},{1,9},{5... | collective-permute-start | bytes 1179656 | tf_op jit(solution)/shard_map/ppermute | solution.py:48
  127.6 21.8 %collective-permute-start.25 = (bf16[256,1024]{1,0:T(8,128)(2,1)S(1)}, bf16[256,1024]{1,0:T(8,128)(2,1)S(1)}, u32[]{:S(2)}, u32[]{:S(2)}) collective-permute-start(bf16[256,1024]{1,0:T(8,128)(2,1)S(1)} %add_convert_fusion.3), channel_id=1, source_target_pairs={{0,2},{1,3},{2,0},{3,1},{4,6},{5,7},{6,4},{7,5},{8,10},{9,11},{10,... | collective-permute-start | bytes 1572872 | tf_op jit(solution)/shard_map/ppermute | solution.py:44
  181.6 24.8 %collective-permute-start.32 = (bf16[256,1024]{1,0:T(8,128)(2,1)S(1)}, bf16[256,1024]{1,0:T(8,128)(2,1)S(1)}, u32[]{:S(2)}, u32[]{:S(2)}) collective-permute-start(bf16[256,1024]{1,0:T(8,128)(2,1)S(1)} %get-tuple-element.97), channel_id=1, source_target_pairs={{0,1},{1,0},{2,3},{3,2},{4,5},{5,4},{6,7},{7,6},{8,9},{9,8},{10,11... | collective-permute-start | bytes 1572872 | tf_op jit(solution)/shard_map/ppermute | solution.py:44
  182.2 19.0 %collective-permute-start.42 = (bf16[128,1536]{1,0:T(8,128)(2,1)S(1)}, bf16[128,1536]{1,0:T(8,128)(2,1)S(1)}, u32[]{:S(2)}, u32[]{:S(2)}) collective-permute-start(bf16[128,1536]{1,0:T(8,128)(2,1)S(1)} %pad_maximum_fusion.3), channel_id=1, source_target_pairs={{0,4},{4,0},{8,12},{12,8},{16,20},{20,16},{24,28},{28,24},{1,5},{5... | collective-permute-start | bytes 1179656 | tf_op jit(solution)/shard_map/ppermute | solution.py:44
  192.9 19.1 %collective-permute-start.44 = (bf16[128,1536]{1,0:T(8,128)(2,1)S(1)}, bf16[128,1536]{1,0:T(8,128)(2,1)S(1)}, u32[]{:S(2)}, u32[]{:S(2)}) collective-permute-start(bf16[128,1536]{1,0:T(8,128)(2,1)S(1)} %pad_maximum_fusion.4), channel_id=1, source_target_pairs={{0,4},{4,0},{8,12},{12,8},{16,20},{20,16},{24,28},{28,24},{1,5},{5... | collective-permute-start | bytes 1179656 | tf_op jit(solution)/shard_map/ppermute | solution.py:44
  205.6 16.9 %collective-permute-start.61 = (bf16[128,1536]{1,0:T(8,128)(2,1)}, bf16[128,1536]{1,0:T(8,128)(2,1)}, u32[]{:S(2)}, u32[]{:S(2)}) collective-permute-start(bf16[128,1536]{1,0:T(8,128)(2,1)} %pad_maximum_fusion.5), channel_id=1, source_target_pairs={{0,4},{4,0},{8,12},{12,8},{16,20},{20,16},{24,28},{28,24},{1,5},{5... | collective-permute-start | bytes 1179656 | tf_op jit(solution)/shard_map/ppermute | solution.py:44
  240.3 103.8 %collective-permute-start.38 = (bf16[512,1024]{1,0:T(8,128)(2,1)}, bf16[512,1024]{1,0:T(8,128)(2,1)}, u32[]{:S(2)}, u32[]{:S(2)}) collective-permute-start(bf16[512,1024]{1,0:T(8,128)(2,1)} %get-tuple-element.102), channel_id=1, source_target_pairs={{0,1},{1,0},{2,3},{3,2},{4,5},{5,4},{6,7},{7,6},{8,9},{9,8},{10,11... | collective-permute-start | bytes 3145736 | tf_op jit(solution)/shard_map/ppermute | solution.py:44
  275.7 29.0 %collective-permute-start.50 = (bf16[128,768]{1,0:T(8,128)(2,1)}, bf16[128,768]{1,0:T(8,128)(2,1)}, u32[]{:S(2)}, u32[]{:S(2)}) collective-permute-start(bf16[128,768]{1,0:T(8,128)(2,1)} %get-tuple-element.257), channel_id=1, source_target_pairs={{0,4},{4,0},{8,12},{12,8},{16,20},{20,16},{24,28},{28,24},{1,5},{5... | collective-permute-start | bytes 589832 | tf_op jit(solution)/shard_map/ppermute | solution.py:44
  276.4 29.7 %collective-permute-start.49 = (bf16[128,768]{1,0:T(8,128)(2,1)}, bf16[128,768]{1,0:T(8,128)(2,1)}, u32[]{:S(2)}, u32[]{:S(2)}) collective-permute-start(bf16[128,768]{1,0:T(8,128)(2,1)} %get-tuple-element.258), channel_id=1, source_target_pairs={{0,4},{4,0},{8,12},{12,8},{16,20},{20,16},{24,28},{28,24},{1,5},{5... | collective-permute-start | bytes 589832 | tf_op jit(solution)/shard_map/ppermute | solution.py:44
  277.8 38.7 %collective-permute-start.48 = (bf16[128,768]{1,0:T(8,128)(2,1)}, bf16[128,768]{1,0:T(8,128)(2,1)}, u32[]{:S(2)}, u32[]{:S(2)}) collective-permute-start(bf16[128,768]{1,0:T(8,128)(2,1)} %get-tuple-element.259), channel_id=1, source_target_pairs={{0,4},{4,0},{8,12},{12,8},{16,20},{20,16},{24,28},{28,24},{1,5},{5... | collective-permute-start | bytes 589832 | tf_op jit(solution)/shard_map/ppermute | solution.py:44
  306.1 18.6 %collective-permute-start.56 = (bf16[128,1152]{1,0:T(8,128)(2,1)}, bf16[128,1152]{1,0:T(8,128)(2,1)}, u32[]{:S(2)}, u32[]{:S(2)}) collective-permute-start(bf16[128,1152]{1,0:T(8,128)(2,1)} %pad_maximum_fusion.8), channel_id=1, source_target_pairs={{0,4},{4,0},{8,12},{12,8},{16,20},{20,16},{24,28},{28,24},{1,5},{5... | collective-permute-start | bytes 884744 | tf_op jit(solution)/shard_map/ppermute | solution.py:44
  316.5 18.7 %collective-permute-start.47 = (bf16[128,768]{1,0:T(8,128)(2,1)}, bf16[128,768]{1,0:T(8,128)(2,1)S(1)}, u32[]{:S(2)}, u32[]{:S(2)}) collective-permute-start(bf16[128,768]{1,0:T(8,128)(2,1)} %get-tuple-element.256), channel_id=1, source_target_pairs={{0,4},{4,0},{8,12},{12,8},{16,20},{20,16},{24,28},{28,24},{1,5},{5... | collective-permute-start | bytes 589832 | tf_op jit(solution)/shard_map/ppermute | solution.py:44
  322.8 14.3 %collective-permute-start.55 = (bf16[128,1152]{1,0:T(8,128)(2,1)}, bf16[128,1152]{1,0:T(8,128)(2,1)}, u32[]{:S(2)}, u32[]{:S(2)}) collective-permute-start(bf16[128,1152]{1,0:T(8,128)(2,1)} %pad_maximum_fusion.7), channel_id=1, source_target_pairs={{0,4},{4,0},{8,12},{12,8},{16,20},{20,16},{24,28},{28,24},{1,5},{5... | collective-permute-start | bytes 884744 | tf_op jit(solution)/shard_map/ppermute | solution.py:44
  357.0 15.4 %collective-permute-start.65 = (f32[2,32,384]{2,1,0:T(8,128)S(1)}, f32[2,32,384]{2,1,0:T(8,128)}, u32[]{:S(2)}, u32[]{:S(2)}) collective-permute-start(f32[2,32,384]{2,1,0:T(8,128)S(1)} %select_bitcast_fusion), channel_id=1, source_target_pairs={{0,1},{1,0},{2,3},{3,2},{4,5},{5,4},{6,7},{7,6},{8,9},{9,8},{10,11... | collective-permute-start | bytes 294920 | tf_op jit(solution)/shard_map/ppermute | solution.py:44
  (173 other events, 2002.6 us)
